TPU v7x, 256 devices: a whole 4x4x8 slice. The times are simulated.
256 devices in a mesh: dp: 32 (over x, z), mp: 8 (over y, core).
Axes of the slice: x: 4, y: 4, z: 8, core: 2. Of those that a mesh axis runs over, the one named last changes fastest.
Arguments:
- activations: bfloat16 [4096, 4096], P('dp', 'mp'), may hold values from -6 to 6
- cotangents: bfloat16 [4096, 16384], P('dp', 'mp'), may hold values from -0.21875 to 0.21875
- owners: int32 [256, 1], P('mp'), may hold values from 0 to 31; in each aligned block of 32 rows (0 to 31, 32 to 63, ...) at most 2 rows name the same one
- stats_left: float32 [8, 32, 2, 512, 512], P('mp', 'dp'), as said below
- stats_right: float32 [8, 32, 2, 512, 512], P('mp', 'dp'), as said below
- variance: float32 [8, 512, 32, 512], P('mp', 'dp'), may hold values from 0.3 to 90, as said below
Outputs:
- direction: bfloat16 [8, 512, 32, 512], P('mp', 'dp')
- new_left: float32 [8, 32, 2, 512, 512], P('mp', 'dp')
- new_right: float32 [8, 32, 2, 512, 512], P('mp', 'dp')
- new_variance: float32 [8, 512, 32, 512], P('mp', 'dp')
Inputs may be any that keep to these rules, and one draw needn't show every extreme that they name: `owners`: among the 32 blocks of one index of mp no owner has more than 2 blocks, and some owner has exactly 2. `stats_left`: every slot is a symmetric positive definite matrix. `stats_right`: every slot is a symmetric positive definite matrix. `variance`: every entry is positive.
All inputs are finite; a program needn't handle non-finite values. Where the computation divides by a largest or mean magnitude, that divisor is 1e-20 or more.
Results may differ from a plain program's by a relative error of at most 0.001.
Values may be sent and summed in bfloat16 or wider, within the bound.
A program may use at most 192 MiB of HBM per device.

v0:
```python
import jax
import jax.numpy as jnp
from jax import lax
from jax.sharding import PartitionSpec as P

ITERS = 2


def batch_product(left_matrix, right_matrix):
    return jnp.einsum(
        "...ij,...jk->...ik", left_matrix, right_matrix, precision=lax.Precision.HIGHEST
    )


def slot_numbers(owner_ids):
    count = owner_ids.shape[-1]
    matching = owner_ids[..., :, None] == owner_ids[..., None, :]
    earlier = jnp.arange(count)[None, :] < jnp.arange(count)[:, None]
    return jnp.sum(jnp.logical_and(matching, earlier), axis=-1)


def inverse_root(statistic, iterations):
    order = statistic.shape[-1]
    identity = jnp.eye(order, dtype=jnp.float32)
    bound = jnp.max(jnp.sum(jnp.abs(statistic), axis=-1), axis=-1)
    matrix = statistic / bound[..., None, None]
    result = identity
    for iteration in range(iterations):
        factor = (5.0 * identity - matrix) * 0.25
        result = factor if iteration == 0 else batch_product(result, factor)
        if iteration + 1 < iterations:
            square = batch_product(factor, factor)
            fourth = batch_product(square, square)
            matrix = batch_product(fourth, matrix)
    return result


def per_device(activations, cotangents, owners, stats_left, stats_right, variance):
    devices_dp = lax.axis_size("dp")
    block_size = stats_left.shape[-1]
    capacity = stats_left.shape[2]
    block_count = owners.shape[0]
    col_count = cotangents.shape[1] // block_size
    row_count = block_count // col_count
    strip_rows = block_size // devices_dp
    token_count = cotangents.shape[0]
    slot_total = devices_dp * capacity
    owner_ids = owners[:, 0]
    slot_ids = slot_numbers(owner_ids)
    targets = owner_ids * capacity + slot_ids
    select = (targets[:, None] == jnp.arange(slot_total, dtype=jnp.int32)[None, :]).astype(
        jnp.float32
    )
    roots = inverse_root(jnp.stack([stats_left[0, 0], stats_right[0, 0]]), ITERS)
    features = lax.all_gather(activations, "mp", axis=1, tiled=True)
    feature_blocks = features.reshape(token_count, row_count, block_size)
    cot_blocks = cotangents.reshape(token_count, col_count, block_size)
    product = jnp.einsum(
        "tir,tjc->rijc", feature_blocks, cot_blocks, preferred_element_type=jnp.float32
    )
    grad_strip = lax.psum_scatter(
        product.reshape(strip_rows * lax.axis_size("dp"), block_count, block_size),
        "dp",
        scatter_dimension=0,
        tiled=True,
    )
    outgoing = jnp.einsum("rbc,bq->qrc", grad_strip, select, precision=lax.Precision.HIGHEST)
    owned_grad = lax.all_to_all(outgoing, "dp", split_axis=0, concat_axis=1, tiled=True)
    precond = batch_product(batch_product(roots[0], owned_grad), roots[1])
    returned = lax.all_to_all(precond, "dp", split_axis=1, concat_axis=0, tiled=True)
    pre_strip = jnp.einsum("qrc,bq->rbc", returned, select, precision=lax.Precision.HIGHEST)
    var_new = 0.9 * variance[0] + 0.1 * grad_strip * grad_strip
    adam_strip = grad_strip / jnp.sqrt(var_new)
    sums_adam, sums_pre = lax.psum(
        (
            jnp.sum(adam_strip * adam_strip, axis=(0, 2)),
            jnp.sum(pre_strip * pre_strip, axis=(0, 2)),
        ),
        "dp",
    )
    entries_per_block = block_size * block_size
    ratio = jnp.sqrt(sums_adam / entries_per_block / (sums_pre / entries_per_block + 1e-06))
    direction = (pre_strip * ratio[None, :, None]).astype(jnp.bfloat16)
    outer_left = batch_product(owned_grad, jnp.swapaxes(owned_grad, -1, -2))
    outer_right = batch_product(jnp.swapaxes(owned_grad, -1, -2), owned_grad)
    left_new = 0.9 * stats_left + 0.1 * outer_left[None, None]
    right_new = 0.9 * stats_right + 0.1 * outer_right[None, None]
    return (direction[None], left_new, right_new, var_new[None])


def solution(mesh):
    return jax.shard_map(
        per_device,
        mesh=mesh,
        in_specs=(
            P("dp", "mp"),
            P("dp", "mp"),
            P("mp", None),
            P("mp", "dp", None, None, None),
            P("mp", "dp", None, None, None),
            P("mp", "dp", None, None),
        ),
        out_specs=(
            P("mp", "dp", None, None),
            P("mp", "dp", None, None, None),
            P("mp", "dp", None, None, None),
            P("mp", "dp", None, None),
        ),
        check_vma=False,
    )
```

profile of v0, /device:TPU:8, one launch (start us, length us, event | category | flops | bytes accessed | tf_op | source)
XLA Modules:
  0.0 625.1 jit_solution(9806855738034789742)
XLA Ops:
  7.2 0.0 all-gather.2.cloned.1.call-start
  7.2 1.7 copy.36
  8.9 0.0 all-gather.2.cloned.1.call-update
  8.9 0.0 reduce-scatter.2.cloned.1.call-start
  8.9 1.3 copy.51
  10.3 27.3 %all-gather.2.cloned.1.call-done = bf16[128,4096]{0,1:T(8,128)(2,1)} async-done(((bf16[128,512]{0,1:T(8,128)(2,1)}), bf16[128,4096]{0,1:T(8,128)(2,1)}) %all-gather.2.cloned.1.call-update) | async-done | bytes 1048592 | tf_op jit(solution)/shard_map/all_gather | solution.py:55
  37.6 16.8 %convolution_bitcast_fusion = f32[512,8,4,512]{0,3,1,2:T(8,128)} fusion(bf16[128,4,512,1]{0,2,3,1:T(8,128)(2,1)S(1)} %bitcast.84, bf16[128,8,512,1]{0,2,1,3:T(8,128)(2,1)} %bitcast.85), kind=kOutput, calls=%fused_computation | convolution fusion | flops 2147483648 | bytes 35127296 | tf_op jit(solution)/shard_map/tir,tjc->rijc/dot_general | solution.py:58
  54.4 33.7 %copy.39 = f32[512,8,4,512]{3,0,2,1:T(8,128)} copy(f32[512,8,4,512]{0,3,1,2:T(8,128)} %convolution_bitcast_fusion) | data formatting | bytes 67108864 | tf_op jit(solution)/shard_map/tir,tjc->rijc/transpose | solution.py:58
  88.2 0.0 copy-start.7
  88.2 0.0 reduce-scatter.2.cloned.1.call-update
  88.2 0.6 copy-done.7
  88.8 0.2 convert_reduce_fusion
  89.0 314.7 %reduce-scatter.2.cloned.1.call-done = f32[16,32,512]{2,0,1:T(8,128)} async-done(((f32[512,32,512]{2,0,1:T(8,128)}), f32[16,32,512]{2,0,1:T(8,128)}) %reduce-scatter.2.cloned.1.call-update) | async-done | bytes 1048592 | tf_op jit(solution)/shard_map/reduce_scatter | solution.py:61
  403.7 2.9 fusion.12
  406.5 2.5 copy.41
  409.1 7.3 %all-to-all-start = ((f32[64,16,512]{2,1,0:T(8,128)}), f32[64,16,512]{2,1,0:T(8,128)S(1)}, u32[]{:S(2)}, u32[]{:S(2)}) async-start(f32[64,16,512]{2,1,0:T(8,128)} %copy.41), calls=%async_computation.1 | async-start | bytes 4194304 | tf_op jit(solution)/shard_map/all_to_all | solution.py:68
  416.4 2.6 abs_reduce_fusion
  419.0 0.1 reduce_max.9
  419.1 0.1 fusion.14
  419.2 11.6 %fusion.3 = f32[2,2,512,512]{3,2,1,0:T(8,128)S(1)} fusion(f32[512,512]{1,0:T(8,128)S(1)} %fusion.14, f32[1,2,512,512]{3,2,1,0:T(8,128)} %bitcast.81, f32[1,2,512,512]{3,2,1,0:T(8,128)} %bitcast.77, f32[2,2]{1,0:T(2,128)S(1)} %reduce_max.9), kind=kOutput, calls=%fused_computation.7 | convolution fusion | flops 6446645248 | bytes 9437200 | tf_op jit(solution)/shard_map/...ij,...jk->...ik/dot_general | solution.py:10
  430.8 0.0 copy-start.1
  430.8 0.0 copy-start.3
  430.8 7.1 %fusion.32 = f32[2,2,512,512]{3,2,1,0:T(8,128)S(1)} fusion(f32[2,2,512,512]{3,2,1,0:T(8,128)S(1)} %fusion.3), kind=kOutput, calls=%fused_computation.47 | convolution fusion | flops 6442450944 | bytes 8388608 | tf_op jit(solution)/shard_map/...ij,...jk->...ik/dot_general | solution.py:10
  437.9 0.0 copy-done.1
  437.9 0.0 copy-done.3
  437.9 7.9 %fusion.29 = f32[2,2,512,512]{3,2,1,0:T(8,128)S(1)} fusion(f32[2,2,512,512]{3,2,1,0:T(8,128)S(1)} %fusion.32, f32[1,2,512,512]{3,2,1,0:T(8,128)S(1)} %bitcast.82, f32[1,2,512,512]{3,2,1,0:T(8,128)S(1)} %bitcast.78, f32[2,2]{1,0:T(2,128)S(1)} %reduce_max.9), kind=kOutput, calls=%fused_computation.46 | convolution fusion | flops 6444548096 | bytes 12582928 | tf_op jit(solution)/shard_map/...ij,...jk->...ik/dot_general | solution.py:10
  445.9 9.3 %fusion = f32[2,2,512,512]{3,2,1,0:T(8,128)} fusion(f32[2,2,512,512]{3,2,1,0:T(8,128)S(1)} %fusion.29, f32[512,512]{1,0:T(8,128)S(1)} %fusion.14, f32[1,2,512,512]{3,2,1,0:T(8,128)S(1)} %bitcast.83, f32[1,2,512,512]{3,2,1,0:T(8,128)S(1)} %bitcast.79, f32[2,2]{1,0:T(2,128)S(1)} %reduce_max.9), kind=kOutput, calls=%fused_computation.2 | convolution fusion | flops 6448742400 | bytes 13631504 | tf_op jit(solution)/shard_map/...ij,...jk->...ik/dot_general | solution.py:10
  455.2 11.2 %all-to-all-done = f32[64,16,512]{2,1,0:T(8,128)S(1)} async-done(((f32[64,16,512]{2,1,0:T(8,128)}), f32[64,16,512]{2,1,0:T(8,128)S(1)}, u32[]{:S(2)}, u32[]{:S(2)}) %all-to-all-start) | async-done | bytes 2097184 | tf_op jit(solution)/shard_map/all_to_all | solution.py:68
  466.4 0.0 copy-start
  466.4 1.3 copy-done
  467.7 0.0 copy-start.5
  467.7 1.9 copy.42
  469.6 0.9 copy-done.5
  470.5 3.5 fusion.6
  474.0 3.5 fusion.5
  477.6 2.9 copy.43
  480.5 0.0 copy-start.6
  480.5 6.6 %all-to-all-start.1 = ((f32[2,512,512]{2,0,1:T(2,128)}), f32[2,512,512]{2,0,1:T(2,128)}, u32[]{:S(2)}, u32[]{:S(2)}) async-start(f32[2,512,512]{2,0,1:T(2,128)} %copy.43), calls=%async_computation.2 | async-start | bytes 4194304 | tf_op jit(solution)/shard_map/all_to_all | solution.py:70
  487.1 0.0 copy-done.6
  487.1 0.0 copy-start.2
  487.1 2.3 fusion.16
  489.4 1.6 copy.47
  491.0 0.0 copy-done.2
  491.0 0.0 copy-start.4
  491.0 5.0 bitcast_add_fusion.1
  496.0 0.0 copy-done.4
  496.0 5.0 bitcast_add_fusion
  501.0 35.8 %all-to-all-done.1 = f32[2,512,512]{2,0,1:T(2,128)} async-done(((f32[2,512,512]{2,0,1:T(2,128)}), f32[2,512,512]{2,0,1:T(2,128)}, u32[]{:S(2)}, u32[]{:S(2)}) %all-to-all-start.1) | async-done | bytes 2097184 | tf_op jit(solution)/shard_map/all_to_all | solution.py:70
  536.8 4.0 copy.63
  540.8 2.7 all_to_all.33
  543.5 1.1 multiply_reduce_fusion
  544.6 72.5 %all-reduce = (f32[32]{0:T(128)S(1)}, f32[32]{0:T(128)S(1)}) all-reduce(f32[32]{0:T(128)S(1)} %get-tuple-element.20, f32[32]{0:T(128)S(1)} %get-tuple-element.19), channel_id=1, replica_groups=mesh['dp'=32,'mp'=8] {'dp'}, use_global_device_ids=true, to_apply=%region_7.0 | all-reduce | flops 64 | bytes 512 | tf_op jit(solution)/shard_map/psum | solution.py:74
  617.1 1.0 fusion.15
  (2 shorter events, 0.0 us)
Async XLA Ops:
  7.2 30.4 %all-gather.2.cloned.1.call-start = ((), (), s32[]{:S(2)}) async-start(), calls=%async_computation.3 | async-start | bytes 1179648 | tf_op jit(solution)/shard_map/all_gather | solution.py:55
  8.9 394.8 %reduce-scatter.2.cloned.1.call-start = ((), (), s32[]{:S(2)}) async-start(), calls=%async_computation.4 | async-start | bytes 34603008 | tf_op jit(solution)/shard_map/reduce_scatter | solution.py:61
  88.2 0.7 copy-start.7
  409.1 57.3 %all-to-all-start = ((f32[64,16,512]{2,1,0:T(8,128)}), f32[64,16,512]{2,1,0:T(8,128)S(1)}, u32[]{:S(2)}, u32[]{:S(2)}) async-start(f32[64,16,512]{2,1,0:T(8,128)} %copy.41), calls=%async_computation.1 | async-start | bytes 4194304 | tf_op jit(solution)/shard_map/all_to_all | solution.py:68
  430.8 7.1 %copy-start.1 = (f32[1,1,2,512,512]{4,3,2,1,0:T(8,128)S(1)}, f32[1,1,2,512,512]{4,3,2,1,0:T(8,128)}, u32[]{:S(2)}) copy-start(f32[1,1,2,512,512]{4,3,2,1,0:T(8,128)} %param.9) | copy-start | bytes 6291460
  430.8 7.1 %copy-start.3 = (f32[1,1,2,512,512]{4,3,2,1,0:T(8,128)S(1)}, f32[1,1,2,512,512]{4,3,2,1,0:T(8,128)}, u32[]{:S(2)}) copy-start(f32[1,1,2,512,512]{4,3,2,1,0:T(8,128)} %param.10) | copy-start | bytes 6291460
  466.4 1.3 copy-start
  467.7 2.8 copy-start.5
  480.5 6.6 %copy-start.6 = (f32[16,32,512]{2,0,1:T(8,128)S(1)}, f32[16,32,512]{2,0,1:T(8,128)}, u32[]{:S(2)}) copy-start(f32[16,32,512]{2,0,1:T(8,128)} %reduce-scatter.2.cloned.1.call-done) | copy-start | bytes 3145732
  480.5 56.3 %all-to-all-start.1 = ((f32[2,512,512]{2,0,1:T(2,128)}), f32[2,512,512]{2,0,1:T(2,128)}, u32[]{:S(2)}, u32[]{:S(2)}) async-start(f32[2,512,512]{2,0,1:T(2,128)} %copy.43), calls=%async_computation.2 | async-start | bytes 4194304 | tf_op jit(solution)/shard_map/all_to_all | solution.py:70
  487.1 3.9 copy-start.2
  491.0 5.0 copy-start.4
Sparse Core Ops, SparseCore 0:
  10.4 27.1 all-gather.1
  88.3 315.2 reduce-scatter.1
where the time goes:
time: 633 us; the launch traced here: 625 us
  waiting for transfers between devices  389 us (61%)
  matrix products  73.7 us (12%)
  blocking collectives  72.5 us (11%)
  local copies, waits for them, and re-layouts  55.2 us (9%)
  between operations  14.4 us (2%)
  starting transfers between devices  13.9 us (2%)
    reduce_scatter x1, waiting for transfers between devices, per_device(): lax.psum_scatter(product.reshape(strip_rows * lax.axis_size('dp'), block_...  315 us
    psum x1, blocking collectives, per_device(): lax.psum((jnp.sum(adam_strip * adam_strip, axis=(0, 2)), jnp.sum(pre_stri...  72.5 us
    dot_general x8, matrix products, batch_product(): jnp.einsum('...ij,...jk->...ik', left_matrix, right_matrix, precision=lax...  53 us
    all_to_all x1, waiting for transfers between devices, per_device(): lax.all_to_all(precond, 'dp', split_axis=1, concat_axis=0, tiled=True)  35.8 us
    transpose x1, local copies, waits for them, and re-layouts, per_device(): jnp.einsum('tir,tjc->rijc', feature_blocks, cot_blocks, preferred_element...  33.7 us
    all_gather x1, waiting for transfers between devices, per_device(): features = lax.all_gather(activations, 'mp', axis=1, tiled=True)  27.3 us
    dot_general x1, matrix products, per_device(): jnp.einsum('tir,tjc->rijc', feature_blocks, cot_blocks, preferred_element...  16.8 us
  transfers between devices with their start and end apart: 4, of which 4 were waited for; matrix products, arithmetic and copies ran while one was open for 9% of the time, Pallas kernels for 0%

commit v1 on v0

v1 whole, which is shorter than its diff:
```python
import jax
import jax.numpy as jnp
from jax import lax
from jax.sharding import Mesh, PartitionSpec as P

X, Z, Y = 4, 8, 4
HIGH = lax.Precision.HIGH


def product(left, right):
    return jnp.einsum("...ij,...jk->...ik", left, right, precision=HIGH)


def root_of(statistic):
    order = statistic.shape[-1]
    identity = jnp.eye(order, dtype=jnp.float32)
    bound = jnp.max(jnp.sum(jnp.abs(statistic), axis=-1), axis=-1)
    factor = 1.25 * identity - statistic * (0.25 / bound)[..., None, None]
    square = product(factor, factor)
    cubic = product(square, 4.0 * square - 5.0 * factor)
    return 1.25 * factor + 0.25 * product(square, cubic)


def slot_targets(owner_ids, capacity):
    count = owner_ids.shape[-1]
    matching = owner_ids[:, None] == owner_ids[None, :]
    earlier = jnp.arange(count)[None, :] < jnp.arange(count)[:, None]
    slots = jnp.sum(jnp.logical_and(matching, earlier), axis=-1)
    return owner_ids * capacity + slots


def per_device(activations, cotangents, owners, stats_left, stats_right, variance):
    tokens, block = activations.shape
    columns = cotangents.shape[1] // block
    count = owners.shape[0]
    rows = count // columns
    capacity = stats_left.shape[2]
    devices = X * Z
    strip = block // devices

    targets = slot_targets(owners[:, 0], capacity)
    slot_ids = jnp.arange(devices * capacity, dtype=jnp.int32)
    select = targets[:, None] == slot_ids[None, :]

    left_root = root_of(stats_left[0, 0])
    right_root = root_of(stats_right[0, 0])

    cot = cotangents.reshape(tokens, columns, block).transpose(1, 0, 2)
    cot = lax.all_to_all(cot, "x", 0, 0, tiled=True)
    cot = lax.all_gather(cot.reshape(X * tokens, block), "z", axis=0, tiled=True)

    act = activations.T.reshape(X, Z, strip, tokens).transpose(1, 0, 2, 3)
    act = lax.all_to_all(act, "z", 0, 0, tiled=True)
    act = act.reshape(Z, X * strip, tokens)
    act = lax.all_gather(act, ("x", "y", "c"), axis=0, tiled=False)
    act = act.reshape(X, rows, Z, X * strip, tokens)
    cot = cot.reshape(Z, X, tokens, block)
    grad = jnp.einsum("xizrt,zxtc->irc", act, cot, preferred_element_type=jnp.float32)

    grad = grad.reshape(rows, X, strip, block).transpose(1, 0, 2, 3)
    grad = lax.all_to_all(grad, "x", 0, 0, tiled=True)
    grad = grad.transpose(2, 1, 0, 3).reshape(strip, count, block)

    var_new = 0.9 * variance[0] + 0.1 * grad * grad
    sums_adam = jnp.sum(grad * grad / var_new, axis=(0, 2))

    outgoing = jnp.einsum(
        "rbc,bq->qrc", grad, select.astype(jnp.float32), precision=lax.Precision.HIGHEST
    )
    scale = jnp.maximum(jnp.max(jnp.abs(outgoing), axis=-1, keepdims=True), 1e-30)
    coded = outgoing * (32767.0 / scale)
    coded = jnp.round(coded).astype(jnp.int16)
    sums_slot = jnp.sum(jnp.where(select, sums_adam[:, None], 0.0), axis=0)
    extra = jnp.concatenate([scale[:, :, 0], sums_slot[:, None]], axis=1)
    coded = lax.all_to_all(coded, ("x", "z"), 0, 0, tiled=True)
    extra = lax.all_to_all(extra, ("x", "z"), 0, 0, tiled=True)
    coded = coded.reshape(devices, capacity, strip, block).transpose(1, 0, 2, 3)
    extra = extra.reshape(devices, capacity, strip + 1).transpose(1, 0, 2)
    scale = extra[:, :, :strip] * (1.0 / 32767.0)
    owned = coded.astype(jnp.float32) * scale[..., None]
    owned = owned.reshape(capacity, block, block)

    precond = product(product(left_root, owned), right_root)
    mean_adam = jnp.sum(extra[:, :, strip], axis=1) / (block * block)
    mean_pre = jnp.mean(precond * precond, axis=(1, 2))
    ratio = jnp.sqrt(mean_adam / (mean_pre + 1e-6))
    finished = (precond * ratio[:, None, None]).astype(jnp.bfloat16)
    finished = finished.reshape(capacity, devices, strip, block).transpose(1, 0, 2, 3)
    finished = lax.all_to_all(finished, ("x", "z"), 0, 0, tiled=True)
    finished = finished.reshape(devices * capacity, strip, block)
    direction = jnp.einsum("qrc,bq->rbc", finished, select.astype(jnp.bfloat16))

    flipped = jnp.swapaxes(owned, -1, -2)
    left_new = 0.9 * stats_left + 0.1 * product(owned, flipped)[None, None]
    right_new = 0.9 * stats_right + 0.1 * product(flipped, owned)[None, None]
    return (direction[None], left_new, right_new, var_new[None])


def solution(mesh):
    fine = Mesh(mesh.devices.reshape(X, Z, Y, 2), ("x", "z", "y", "c"))
    dp, mp = ("x", "z"), ("y", "c")

    def whole(activations, cotangents, owners, stats_left, stats_right, variance):
        return per_device(activations, cotangents, owners, stats_left, stats_right, variance)

    return jax.shard_map(
        whole,
        mesh=fine,
        in_specs=(
            P(dp, mp),
            P(dp, mp),
            P(mp, None),
            P(mp, dp, None, None, None),
            P(mp, dp, None, None, None),
            P(mp, dp, None, None),
        ),
        out_specs=(
            P(mp, dp, None, None),
            P(mp, dp, None, None, None),
            P(mp, dp, None, None, None),
            P(mp, dp, None, None),
        ),
        check_vma=False,
    )
```

time: 633 us -> 269 us (0.42); the launches traced: 625 us -> 268 us
  waiting for transfers between devices: 389 us -> 131 us
  local copies, waits for them, and re-layouts: 55.2 us -> 13.4 us
  blocking collectives: 72.5 us -> 31.1 us
  matrix products: 73.7 us -> 44.8 us
  starting transfers between devices: 13.9 us -> 22.3 us
    reduce_scatter x1 -> x0, waiting for transfers between devices: 315 us -> none  [per_device(): lax.psum_scatter(product.reshape(strip_rows * lax.axis_size('dp'), block_...]
    psum x1 -> x0, blocking collectives: 72.5 us -> none  [per_device(): lax.psum((jnp.sum(adam_strip * adam_strip, axis=(0, 2)), jnp.sum(pre_stri...]
    all_gather x1 -> x2, waiting for transfers between devices: 27.3 us -> 87.6 us  [the longest x1 51.8 us: per_device(): act = lax.all_gather(act, ('x', 'y', 'c'), axis=0, tiled=False)]
    transpose x1 -> x2, local copies, waits for them, and re-layouts: 33.7 us -> 1.09 us  [the longest x1 1.08 us: per_device(): grad = grad.reshape(rows, X, strip, block).transpose(1, 0, 2, 3)]
    all_to_all x0 -> x2, blocking collectives: none -> 31.1 us  [the longest x1 17.6 us: per_device(): act = lax.all_to_all(act, 'z', 0, 0, tiled=True)]
    dot_general x11 -> x13, matrix products: 73.7 us -> 44.8 us  [the longest x10 33.1 us: product(): return jnp.einsum('...ij,...jk->...ik', left, right, precision=HIGH)]
    all_to_all x2 -> x4, starting transfers between devices: 13.9 us -> 22.2 us  [the longest x1 8.01 us: per_device(): extra = lax.all_to_all(extra, ('x', 'z'), 0, 0, tiled=True)]
    all_to_all x2 -> x4, waiting for transfers between devices: 47 us -> 43.3 us  [the longest x1 16.5 us: per_device(): finished = lax.all_to_all(finished, ('x', 'z'), 0, 0, tiled=True)]
  transfers between devices with their start and end apart: 4 -> 6, of which waited for: 4 -> 6; matrix products, arithmetic and copies ran while one was open for 9% -> 14% of each run, Pallas kernels for 0% -> 0%
where the time goes in v1:
time: 269 us; the launch traced here: 268 us
  waiting for transfers between devices  131 us (49%)
  matrix products  44.8 us (17%)
  blocking collectives  31.1 us (12%)
  starting transfers between devices  22.3 us (8%)
  between operations  14.3 us (5%)
  local copies, waits for them, and re-layouts  13.4 us (5%)
  other arithmetic  11.1 us (4%)
    all_gather x1, waiting for transfers between devices, per_device(): act = lax.all_gather(act, ('x', 'y', 'c'), axis=0, tiled=False)  51.8 us
    all_gather x1, waiting for transfers between devices, per_device(): lax.all_gather(cot.reshape(X * tokens, block), 'z', axis=0, tiled=True)  35.8 us
    dot_general x10, matrix products, product(): return jnp.einsum('...ij,...jk->...ik', left, right, precision=HIGH)  33.1 us
    all_to_all x1, blocking collectives, per_device(): act = lax.all_to_all(act, 'z', 0, 0, tiled=True)  17.6 us
    all_to_all x1, waiting for transfers between devices, per_device(): finished = lax.all_to_all(finished, ('x', 'z'), 0, 0, tiled=True)  16.5 us
    all_to_all x1, blocking collectives, per_device(): cot = lax.all_to_all(cot, 'x', 0, 0, tiled=True)  13.6 us
    all_to_all x1, waiting for transfers between devices, per_device(): coded = lax.all_to_all(coded, ('x', 'z'), 0, 0, tiled=True)  13.5 us
    all_to_all x1, starting transfers between devices, per_device(): extra = lax.all_to_all(extra, ('x', 'z'), 0, 0, tiled=True)  8.01 us
  transfers between devices with their start and end apart: 6, of which 6 were waited for; matrix products, arithmetic and copies ran while one was open for 14% of the time, Pallas kernels for 0%

profile of v1, /device:TPU:8, one launch (start us, length us, event | category | flops | bytes accessed | tf_op | source)
XLA Modules:
  0.0 267.9 jit_solution(7485981725863951092)
XLA Ops:
  7.2 0.0 all-gather.5.cloned.1.call-start
  7.2 1.3 copy.102
  8.6 13.6 %all_to_all.31 = bf16[4,128,512]{1,2,0:T(8,128)(2,1)S(1)} all-to-all(bf16[4,128,512]{1,2,0:T(8,128)(2,1)S(1)} %bitcast.131), channel_id=1, replica_groups=mesh['x'=4,'z'=8,'y'=4,'c'=2] {'x'}, dimensions={0} | all-to-all | bytes 1048576 | tf_op jit(solution)/shard_map/all_to_all | solution.py:49
  22.1 1.0 copy.103
  23.1 0.0 all-gather.5.cloned.1.call-update
  23.2 0.0 all-gather.3.cloned.1.call-start
  23.2 0.1 copy.99
  23.4 17.6 %all_to_all.32 = bf16[8,4,16,128]{3,2,1,0:T(8,128)(2,1)} all-to-all(bf16[8,4,16,128]{3,2,1,0:T(8,128)(2,1)S(1)} %copy.100), channel_id=1, replica_groups=mesh['x'=4,'z'=8,'y'=4,'c'=2] {'z'}, dimensions={0} | all-to-all | bytes 262144 | tf_op jit(solution)/shard_map/all_to_all | solution.py:53
  40.9 0.0 all-gather.3.cloned.1.call-update
  41.0 0.0 copy-start.13
  41.0 1.8 fusion.6
  42.8 0.1 reduce_max.27
  43.0 0.3 fusion.4
  43.2 0.1 reduce_max.29
  43.3 0.2 convert_reduce_fusion
  43.5 35.8 %all-gather.5.cloned.1.call-done = bf16[4096,512]{1,0:T(8,128)(2,1)} async-done(((bf16[512,512]{1,0:T(8,128)(2,1)}), bf16[4096,512]{1,0:T(8,128)(2,1)}) %all-gather.5.cloned.1.call-update) | async-done | bytes 4194320 | tf_op jit(solution)/shard_map/all_gather | solution.py:50
  79.3 51.8 %all-gather.3.cloned.1.call-done = bf16[32,8,64,128]{3,2,1,0:T(8,128)(2,1)} async-done(((bf16[1,8,64,128]{3,2,1,0:T(8,128)(2,1)}), bf16[32,8,64,128]{3,2,1,0:T(8,128)(2,1)}) %all-gather.3.cloned.1.call-update) | async-done | bytes 4194320 | tf_op jit(solution)/shard_map/all_gather | solution.py:55
  131.1 5.4 %fusion.32 = f32[4,8,16,512]{3,2,0,1:T(8,128)S(1)} fusion(bf16[8,4,16,128,4,8]{3,2,1,5,0,4:T(8,128)(2,1)} %bitcast.138, bf16[8,4,128,512,1,1]{3,2,1,0,5,4:T(8,128)(2,1)} %bitcast.137), kind=kOutput, calls=%fused_computation.39 | convolution fusion | flops 2147483648 | bytes 9437184 | tf_op jit(solution)/shard_map/xizrt,zxtc->irc/dot_general | solution.py:58
  136.6 1.1 copy.106
  137.6 4.2 %all-to-all-start.2 = ((f32[4,8,16,512]{3,2,1,0:T(8,128)}), f32[4,8,16,512]{3,2,1,0:T(8,128)}, u32[]{:S(2)}, u32[]{:S(2)}) async-start(f32[4,8,16,512]{3,2,1,0:T(8,128)} %copy.106), calls=%async_computation.2 | async-start | bytes 2097152 | tf_op jit(solution)/shard_map/all_to_all | solution.py:61
  141.9 0.1 fusion.62
  142.0 5.5 %fusion.25 = f32[2,512,512]{2,1,0:T(8,128)} fusion(f32[1,1,2,512,512]{4,3,2,1,0:T(8,128)} %param.9, f32[2]{0:T(128)S(1)} %broadcast_divide_fusion.2, f32[512,512]{1,0:T(8,128)S(1)} %fusion.62), kind=kOutput, calls=%fused_computation.35 | convolution fusion | flops 1611661312 | bytes 5242888 | tf_op jit(solution)/shard_map/...ij,...jk->...ik/dot_general | solution.py:11
  147.6 3.3 %fusion.29 = f32[2,512,512]{2,1,0:T(8,128)} fusion(f32[1,1,2,512,512]{4,3,2,1,0:T(8,128)S(1)} %copy-done, f32[2]{0:T(128)S(1)} %broadcast_divide_fusion.1, f32[512,512]{1,0:T(8,128)S(1)} %fusion.62), kind=kOutput, calls=%fused_computation.36 | convolution fusion | flops 1611661312 | bytes 5242888 | tf_op jit(solution)/shard_map/...ij,...jk->...ik/dot_general | solution.py:11
  150.9 6.9 %all-to-all-done.2 = f32[4,8,16,512]{3,2,1,0:T(8,128)} async-done(((f32[4,8,16,512]{3,2,1,0:T(8,128)}), f32[4,8,16,512]{3,2,1,0:T(8,128)}, u32[]{:S(2)}, u32[]{:S(2)}) %all-to-all-start.2) | async-done | bytes 1048608 | tf_op jit(solution)/shard_map/all_to_all | solution.py:61
  157.8 1.4 copy.107
  159.1 0.1 copy-done.11
  159.3 1.8 fusion.37
  161.1 1.6 fusion.61
  162.7 0.1 broadcast_in_dim.12
  162.8 0.1 select_reduce_fusion
  162.8 0.2 concatenate.8
  163.0 4.1 %abs_reduce_fusion = (f32[64,16]{0,1:T(8,128)S(1)}, f32[64,16,512]{2,0,1:T(8,128)}) fusion(f32[16,32,512]{2,0,1:T(8,128)} %bitcast.125, s32[32]{0:T(128)S(1)} %fusion.69), kind=kOutput, calls=%fused_computation.26 | convolution fusion | flops 202376192 | bytes 3149952 | tf_op jit(solution)/shard_map/rbc,bq->qrc/dot_general | solution.py:67
  167.2 0.1 copy.110
  167.3 0.7 pad_maximum_fusion
  168.0 8.0 %all-to-all-start.4 = ((f32[32,2,17]{2,1,0:T(2,128)}), f32[32,2,17]{2,1,0:T(2,128)S(1)}, u32[]{:S(2)}, u32[]{:S(2)}) async-start(f32[32,2,17]{2,1,0:T(2,128)} %pad_maximum_fusion), calls=%async_computation.4 | async-start | bytes 65536 | tf_op jit(solution)/shard_map/all_to_all | solution.py:76
  176.0 2.0 round-nearest-even_convert_fusion
  178.0 1.5 copy.109
  179.5 6.4 %all-to-all-done.4 = f32[32,2,17]{2,1,0:T(2,128)S(1)} async-done(((f32[32,2,17]{2,1,0:T(2,128)}), f32[32,2,17]{2,1,0:T(2,128)S(1)}, u32[]{:S(2)}, u32[]{:S(2)}) %all-to-all-start.4) | async-done | bytes 4384 | tf_op jit(solution)/shard_map/all_to_all | solution.py:76
  185.9 4.9 %all-to-all-start.3 = ((s16[64,16,512]{2,1,0:T(8,128)(2,1)}), s16[64,16,512]{2,1,0:T(8,128)(2,1)}, u32[]{:S(2)}, u32[]{:S(2)}) async-start(s16[64,16,512]{2,1,0:T(8,128)(2,1)} %copy.109), calls=%async_computation.3 | async-start | bytes 2097152 | tf_op jit(solution)/shard_map/all_to_all | solution.py:75
  190.8 4.5 %fusion.11 = f32[2,512,512]{2,1,0:T(8,128)S(1)} fusion(f32[2,512,512]{2,1,0:T(8,128)} %fusion.29, f32[1,1,2,512,512]{4,3,2,1,0:T(8,128)S(1)} %copy-done, f32[2]{0:T(128)S(1)} %broadcast_divide_fusion.1, f32[512,512]{1,0:T(8,128)S(1)} %fusion.62), kind=kOutput, calls=%fused_computation.20 | convolution fusion | flops 1613234176 | bytes 7340040 | tf_op jit(solution)/shard_map/...ij,...jk->...ik/dot_general | solution.py:11
  195.3 0.0 copy-start.3
  195.3 0.0 copy-start.6
  195.3 3.2 %fusion.80 = f32[2,512,512]{2,1,0:T(8,128)} fusion(f32[2,512,512]{2,1,0:T(8,128)S(1)} %copy-done.7, f32[2,512,512]{2,1,0:T(8,128)S(1)} %fusion.11), kind=kOutput, calls=%fused_computation.101 | convolution fusion | flops 1610612736 | bytes 6291456 | tf_op jit(solution)/shard_map/...ij,...jk->...ik/dot_general | solution.py:11
  198.5 2.1 fusion.19
  200.7 3.2 %fusion.79 = f32[2,512,512]{2,1,0:T(8,128)} fusion(f32[2,512,512]{2,1,0:T(8,128)S(1)} %copy-done.6, f32[2,512,512]{2,1,0:T(8,128)S(1)} %fusion.19), kind=kOutput, calls=%fused_computation.100 | convolution fusion | flops 1610612736 | bytes 6291456 | tf_op jit(solution)/shard_map/...ij,...jk->...ik/dot_general | solution.py:11
  203.9 0.2 slice_reduce_fusion
  204.1 13.5 %all-to-all-done.3 = s16[64,16,512]{2,1,0:T(8,128)(2,1)} async-done(((s16[64,16,512]{2,1,0:T(8,128)(2,1)}), s16[64,16,512]{2,1,0:T(8,128)(2,1)}, u32[]{:S(2)}, u32[]{:S(2)}) %all-to-all-start.3) | async-done | bytes 1048608 | tf_op jit(solution)/shard_map/all_to_all | solution.py:75
  217.7 1.6 fusion.3
  219.3 0.3 copy.113
  219.6 1.3 copy-done.4
  220.9 0.6 copy-done.10
  221.5 2.0 fusion.16
  223.6 0.2 copy-done.9
  223.7 2.5 multiply_reduce_fusion
  226.2 0.2 fusion.70
  226.3 0.3 multiply_convert_fusion
  226.7 1.0 copy.143
  227.7 5.1 %all-to-all-start.5 = ((bf16[32,2,16,512]{3,2,1,0:T(8,128)(2,1)}), bf16[32,2,16,512]{3,2,1,0:T(8,128)(2,1)S(1)}, u32[]{:S(2)}, u32[]{:S(2)}) async-start(bf16[32,2,16,512]{3,2,1,0:T(8,128)(2,1)} %bitcast.127), calls=%async_computation.5 | async-start | bytes 2097152 | tf_op jit(solution)/shard_map/all_to_all | solution.py:89
  232.8 0.0 copy-start.2
  232.8 3.0 %copy.117 = f32[1,16,32,512]{3,2,1,0:T(8,128)} copy(f32[1,16,32,512]{3,1,2,0:T(8,128)} %get-tuple-element.20) | data formatting | bytes 2097152
  235.8 3.3 %bitcast_add_fusion = f32[1,1,2,512,512]{4,3,2,1,0:T(8,128)} fusion(f32[1,1,2,512,512]{4,3,2,1,0:T(8,128)S(1)} %copy-done.2, f32[2,512,512]{2,1,0:T(8,128)S(1)} %bitcast.123), kind=kOutput, calls=%fused_computation.5 | convolution fusion | flops 1612185600 | bytes 6291456 | tf_op jit(solution)/shard_map/...ij,...jk->...ik/dot_general | solution.py:11
  239.1 3.3 %bitcast_add_fusion.1 = f32[1,1,2,512,512]{4,3,2,1,0:T(8,128)} fusion(f32[1,1,2,512,512]{4,3,2,1,0:T(8,128)S(1)} %copy-done.5, f32[2,512,512]{2,1,0:T(8,128)S(1)} %bitcast.124), kind=kOutput, calls=%fused_computation.6 | convolution fusion | flops 1612185600 | bytes 6291456 | tf_op jit(solution)/shard_map/...ij,...jk->...ik/dot_general | solution.py:11
  242.4 16.5 %all-to-all-done.5 = bf16[32,2,16,512]{3,2,1,0:T(8,128)(2,1)S(1)} async-done(((bf16[32,2,16,512]{3,2,1,0:T(8,128)(2,1)}), bf16[32,2,16,512]{3,2,1,0:T(8,128)(2,1)S(1)}, u32[]{:S(2)}, u32[]{:S(2)}) %all-to-all-start.5) | async-done | bytes 1048608 | tf_op jit(solution)/shard_map/all_to_all | solution.py:89
  258.9 2.1 convolution_bitcast_fusion
  (26 shorter events, 0.1 us)
Async XLA Ops:
  7.2 16.1 %copy-start.12 = (bf16[128,512]{1,0:T(8,128)(2,1)S(1)}, bf16[128,512]{1,0:T(8,128)(2,1)}, u32[]{:S(2)}) copy-start(bf16[128,512]{1,0:T(8,128)(2,1)} %param.6) | copy-start | bytes 393220
  7.2 72.2 %all-gather.5.cloned.1.call-start = ((), (), s32[]{:S(2)}) async-start(), calls=%async_computation.7 | async-start | bytes 4718592 | tf_op jit(solution)/shard_map/all_gather | solution.py:50
  22.1 20.8 %copy-start = (f32[1,1,2,512,512]{4,3,2,1,0:T(8,128)S(1)}, f32[1,1,2,512,512]{4,3,2,1,0:T(8,128)}, u32[]{:S(2)}) copy-start(f32[1,1,2,512,512]{4,3,2,1,0:T(8,128)} %param.10) | copy-start | bytes 6291460
  23.2 107.9 %all-gather.3.cloned.1.call-start = ((), (), s32[]{:S(2)}) async-start(), calls=%async_computation.6 | async-start | bytes 4325376 | tf_op jit(solution)/shard_map/all_gather | solution.py:55
  41.0 2.4 copy-start.13
  137.6 20.1 %all-to-all-start.2 = ((f32[4,8,16,512]{3,2,1,0:T(8,128)}), f32[4,8,16,512]{3,2,1,0:T(8,128)}, u32[]{:S(2)}, u32[]{:S(2)}) async-start(f32[4,8,16,512]{3,2,1,0:T(8,128)} %copy.106), calls=%async_computation.2 | async-start | bytes 2097152 | tf_op jit(solution)/shard_map/all_to_all | solution.py:61
  157.8 1.5 copy-start.11
  159.3 1.8 copy-start.8
  168.0 17.9 %all-to-all-start.4 = ((f32[32,2,17]{2,1,0:T(2,128)}), f32[32,2,17]{2,1,0:T(2,128)S(1)}, u32[]{:S(2)}, u32[]{:S(2)}) async-start(f32[32,2,17]{2,1,0:T(2,128)} %pad_maximum_fusion), calls=%async_computation.4 | async-start | bytes 65536 | tf_op jit(solution)/shard_map/all_to_all | solution.py:76
  185.9 31.8 %all-to-all-start.3 = ((s16[64,16,512]{2,1,0:T(8,128)(2,1)}), s16[64,16,512]{2,1,0:T(8,128)(2,1)}, u32[]{:S(2)}, u32[]{:S(2)}) async-start(s16[64,16,512]{2,1,0:T(8,128)(2,1)} %copy.109), calls=%async_computation.3 | async-start | bytes 2097152 | tf_op jit(solution)/shard_map/all_to_all | solution.py:75
  190.8 4.5 %copy-start.7 = (f32[2,512,512]{2,1,0:T(8,128)S(1)}, f32[2,512,512]{2,1,0:T(8,128)}, u32[]{:S(2)}) copy-start(f32[2,512,512]{2,1,0:T(8,128)} %fusion.29) | copy-start | bytes 6291460
  195.3 3.2 %copy-start.3 = (f32[1,1,2,512,512]{4,3,2,1,0:T(8,128)S(1)}, f32[1,1,2,512,512]{4,3,2,1,0:T(8,128)}, u32[]{:S(2)}) copy-start(f32[1,1,2,512,512]{4,3,2,1,0:T(8,128)} %param.9) | copy-start | bytes 6291460
  195.3 3.2 %copy-start.6 = (f32[2,512,512]{2,1,0:T(8,128)S(1)}, f32[2,512,512]{2,1,0:T(8,128)}, u32[]{:S(2)}) copy-start(f32[2,512,512]{2,1,0:T(8,128)} %fusion.25) | copy-start | bytes 6291460
  219.3 1.6 copy-start.4
  219.3 2.2 copy-start.10
  221.5 2.1 copy-start.1
  221.5 2.2 copy-start.9
  227.7 31.2 %all-to-all-start.5 = ((bf16[32,2,16,512]{3,2,1,0:T(8,128)(2,1)}), bf16[32,2,16,512]{3,2,1,0:T(8,128)(2,1)S(1)}, u32[]{:S(2)}, u32[]{:S(2)}) async-start(bf16[32,2,16,512]{3,2,1,0:T(8,128)(2,1)} %bitcast.127), calls=%async_computation.5 | async-start | bytes 2097152 | tf_op jit(solution)/shard_map/all_to_all | solution.py:89
  232.8 3.0 %copy-start.2 = (f32[1,1,2,512,512]{4,3,2,1,0:T(8,128)S(1)}, f32[1,1,2,512,512]{4,3,2,1,0:T(8,128)}, u32[]{:S(2)}) copy-start(f32[1,1,2,512,512]{4,3,2,1,0:T(8,128)} %param.10) | copy-start | bytes 6291460
  235.8 3.3 %copy-start.5 = (f32[1,1,2,512,512]{4,3,2,1,0:T(8,128)S(1)}, f32[1,1,2,512,512]{4,3,2,1,0:T(8,128)}, u32[]{:S(2)}) copy-start(f32[1,1,2,512,512]{4,3,2,1,0:T(8,128)} %param.9) | copy-start | bytes 6291460
Sparse Core Ops, SparseCore 0:
  23.3 56.0 all-gather.4
  81.9 49.1 all-gather.2

commit v2 on v1

--- a/solution.py
+++ b/solution.py
@@ -1,24 +1,321 @@
+import functools
+
 import jax
 import jax.numpy as jnp
 from jax import lax
+from jax.experimental import pallas as pl
+from jax.experimental.pallas import tpu as pltpu
 from jax.sharding import Mesh, PartitionSpec as P
 
 X, Z, Y = 4, 8, 4
 HIGH = lax.Precision.HIGH
+MESH = pl.DeviceIdType.MESH
+COEFFICIENTS = (
+    25 / 16, -5 / 16 - 3125 / 4096, 3125 / 4096, -1250 / 4096, 250 / 4096, -25 / 4096, 1 / 4096,
+)
+
+
+def halves(value):
+    high = value.astype(jnp.bfloat16)
+    return high, (value - high.astype(jnp.float32)).astype(jnp.bfloat16)
+
+
+def dot(left, right):
+    return jnp.dot(left, right, preferred_element_type=jnp.float32)
+
+
+def tiled_product(left_high, left_low, right_high, right_low, order, finish):
+    tile = order // 2
+
+    def one(step, carry):
+        rows = pl.ds(pl.multiple_of(step * tile, tile), tile)
+        high, low = left_high[rows, :], left_low[rows, :]
+        total = dot(high, right_low[...]) + dot(low, right_high[...])
+        finish(rows, dot(high, right_high[...]) + total)
+        return carry
+
+    lax.fori_loop(0, 2, one, 0)
+
+
+def gather_kernel(
+    sizes, act, cot, stats_left, stats_right, strips, roots,
+    cbuf, abuf, grad, sbuf, m2, m_h, m_l, m2_h, m2_l, w_h, w_l,
+    own_sem, stat_sem, c1_s, c1_r, a1_s, a1_r, zr_s, zr_r, a2_s, a2_r,
+    y_s, y_r, sib_s, sib_r, ex_s, ex_r,
+):
+    nx, nz, ny, block, strip, tokens, rows_i = sizes
+    half = nz // 2
+    x, z = lax.axis_index("x"), lax.axis_index("z")
+    y, c = lax.axis_index("y"), lax.axis_index("c")
+    mine = 2 * y + c
+
+    def remote(src, dst, send, recv, **where):
+        return pltpu.make_async_remote_copy(
+            src_ref=src, dst_ref=dst, send_sem=send, recv_sem=recv,
+            device_id=where, device_id_type=MESH,
+        )
+
+    loads = [
+        pltpu.make_async_copy(ref.at[slot], sbuf.at[2 * side + slot], stat_sem.at[2 * side + slot])
+        for side, ref in enumerate((stats_left, stats_right))
+        for slot in range(2)
+    ]
+    own_c = pltpu.make_async_copy(
+        cot.at[:, pl.ds(pl.multiple_of(x * block, block), block)], cbuf.at[z, x], own_sem.at[0]
+    )
+    own_a = pltpu.make_async_copy(act.at[z], abuf.at[z, x, mine], own_sem.at[1])
+    own_c.start()
+    own_a.start()
+    for load in loads:
+        load.start()
+
+    barrier = pltpu.get_barrier_semaphore()
+    partners = [{"x": lax.rem(x + d, nx)} for d in range(1, nx)]
+    partners += [{"z": lax.rem(z + d, nz)} for d in range(1, nz)]
+    partners += [{"y": lax.rem(y + d, ny)} for d in range(1, ny)]
+    partners += [{"c": 1 - c}]
+    for partner in partners:
+        pl.semaphore_signal(barrier, inc=1, device_id=partner, device_id_type=MESH)
+    pl.semaphore_wait(barrier, len(partners))
+
+    sends = []
+
+    def launch(copy):
+        copy.start()
+        sends.append(copy)
+
+    def c1(d):
+        j = lax.rem(x + d, nx)
+        return remote(
+            cot.at[:, pl.ds(pl.multiple_of(j * block, block), block)],
+            cbuf.at[z, x], c1_s.at[d - 1], c1_r.at[d - 1], x=j,
+        )
+
+    def a1(d):
+        z2 = lax.rem(z + d, nz)
+        return remote(act.at[z2], abuf.at[z, x, mine], a1_s.at[d - 1], a1_r.at[d - 1], z=z2)
+
+    def ring(way, hop, k):
+        x2 = lax.rem(x - k + nx, nx)
+        step = 1 if way == 0 else nz - 1
+        origin = lax.rem(z - hop + nz, nz) if way == 0 else lax.rem(z + hop, nz)
+        part = cbuf.at[origin, x2]
+        return remote(
+            part, part, zr_s.at[way, hop, k], zr_r.at[way, hop, k], z=lax.rem(z + step, nz)
+        )
+
+    def a2(d):
+        part = abuf.at[:, x, mine]
+        return remote(part, part, a2_s.at[d - 1], a2_r.at[d - 1], x=lax.rem(x + d, nx))
+
+    def over_y(k, d):
+        part = abuf.at[:, lax.rem(x - k + nx, nx), mine]
+        return remote(
+            part, part, y_s.at[k, d - 1], y_r.at[k, d - 1], y=lax.rem(y + d, ny)
+        )
+
+    def sibling(k, d):
+        part = abuf.at[:, lax.rem(x - k + nx, nx), 2 * lax.rem(y - d + ny, ny) + c]
+        return remote(part, part, sib_s.at[k, d], sib_r.at[k, d], c=1 - c)
+
+    for d in range(1, nx):
+        launch(c1(d))
+    own_c.wait()
+    for way in range(2):
+        launch(ring(way, 0, 0))
+    for d in range(1, nz):
+        launch(a1(d))
+    for k in range(1, nx):
+        c1(k).wait_recv()
+        for way in range(2):
+            launch(ring(way, 0, k))
+    own_a.wait()
+    for d in range(1, nz):
+        a1(d).wait_recv()
+    for d in range(1, nx):
+        launch(a2(d))
+    for d in range(1, ny):
+        launch(over_y(0, d))
+    launch(sibling(0, 0))
+    for load in loads:
+        load.wait()
+
+    items = nx * (ny - 1)
+    per_step = -(-items // 6)
+
+    def one_matrix(q, carry):
+        for t in range(3):
+            n = 3 * q + t
+            hop, k = n // nx + 1, lax.rem(n, nx)
+            ring(0, hop - 1, k).wait_recv()
+            ring(1, hop - 1, k).wait_recv()
+            inner = hop < half - 1
+
+            @pl.when(jnp.logical_or(inner, k < nx // 2))
+            def _():
+                ring(0, hop, k).start()
+
+            @pl.when(jnp.logical_or(inner, k >= nx // 2))
+            def _():
+                ring(1, hop, k).start()
+
+            if t + 1 < nx:
+
+                @pl.when(q == 0)
+                def _():
+                    a2(t + 1).wait_recv()
+                    for d in range(1, ny):
+                        over_y(t + 1, d).start()
+                    sibling(t + 1, 0).start()
+
+            for extra in range(per_step):
+                item = (n - 3) * per_step + extra
+
+                @pl.when(jnp.logical_and(n >= 3, item < items))
+                def _():
+                    k2, d2 = item // (ny - 1), lax.rem(item, ny - 1) + 1
+                    over_y(k2, d2).wait_recv()
+                    sibling(k2, d2).start()
+
+            if t == 0:
+                stat = sbuf[q]
+                bound = jnp.max(jnp.sum(jnp.abs(stat), axis=1, keepdims=True), axis=0, keepdims=True)
+                matrix = stat * (1.0 / bound)
+                sbuf[q] = matrix
+                m_h[...], m_l[...] = halves(matrix)
+
+                def finish(rows, value):
+                    m2[rows, :] = value
+                    m2_h[rows, :], m2_l[rows, :] = halves(value)
+                    w_h[rows, :], w_l[rows, :] = halves(
+                        COEFFICIENTS[5] * sbuf[q, rows, :] + COEFFICIENTS[6] * value
+                    )
+
+                tiled_product(m_h, m_l, m_h, m_l, block, finish)
+            elif t == 1:
+
+                def finish(rows, value):
+                    value += COEFFICIENTS[3] * sbuf[q, rows, :] + COEFFICIENTS[4] * m2[rows, :]
+                    m_h[rows, :], m_l[rows, :] = halves(value)
+
+                tiled_product(m2_h, m2_l, w_h, w_l, block, finish)
+            else:
+
+                def finish(rows, value):
+                    value += COEFFICIENTS[1] * sbuf[q, rows, :] + COEFFICIENTS[2] * m2[rows, :]
+                    ids = lax.broadcasted_iota(jnp.int32, value.shape, 0) + rows.start
+                    columns = lax.broadcasted_iota(jnp.int32, value.shape, 1)
+                    roots[q, rows, :] = value + jnp.where(ids == columns, COEFFICIENTS[0], 0.0)
+
+                tiled_product(m2_h, m2_l, m_h, m_l, block, finish)
+        return carry
+
+    lax.fori_loop(0, 4, one_matrix, 0)
+
+    for k in range(nx):
+        for d in range(ny):
+            sibling(k, d).wait_recv()
+
+    def shard(origin, rows=None):
+        parts = []
+        for x2 in range(nx):
+            if rows is None:
+                piece = abuf[origin, x2]
+            else:
+                piece = abuf[origin, x2, :, rows, :]
+            parts.append(piece.reshape(-1, tokens))
+        left = jnp.concatenate(parts, axis=1)
+        return dot(left, cbuf[origin].reshape(nx * tokens, block))
+
+    grad[...] = shard(z).reshape(grad.shape)
+
+    def add(d, carry):
+        grad[...] += shard(lax.rem(z + d + (d >= half).astype(jnp.int32), nz)).reshape(grad.shape)
+        return carry
+
+    lax.fori_loop(1, nz - 1, add, 0)
+
+    for k in range(nx):
+        ring(0 if k < nx // 2 else 1, half - 1, k).wait_recv()
+    far = lax.rem(z + half, nz)
+
+    def exchange(d):
+        j = lax.rem(x + d, nx)
+        rows = pl.ds(pl.multiple_of(j * strip, strip), strip)
+        return rows, remote(
+            grad.at[:, rows, :], strips.at[x], ex_s.at[d - 1], ex_r.at[d - 1], x=j
+        )
+
+    for d in range(1, nx):
+        rows, copy = exchange(d)
+        grad[:, rows, :] += shard(far, rows).reshape(rows_i, strip, block)
+        launch(copy)
+    rows = pl.ds(pl.multiple_of(x * strip, strip), strip)
+    strips[x] = grad[:, rows, :] + shard(far, rows).reshape(rows_i, strip, block)
+    for d in range(1, nx):
+        exchange(d)[1].wait_recv()
+
+    for copy in sends:
+        copy.wait_send()
+    for hop in range(1, half):
+        for k in range(nx):
+            for way in range(2):
+                if hop < half - 1 or (k < nx // 2) == (way == 0):
+                    ring(way, hop, k).wait_send()
+    for k in range(1, nx):
+        for d in range(1, ny):
+            over_y(k, d).wait_send()
+    for k in range(nx):
+        for d in range(ny):
+            if (k, d) != (0, 0):
+                sibling(k, d).wait_send()
+
+
+def gather_and_roots(act, cot, stats_left, stats_right):
+    nz, rows_z, tokens = act.shape
+    nx, ny = lax.axis_size("x"), lax.axis_size("y")
+    block = stats_left.shape[-1]
+    strip = rows_z // nx
+    rows_i = 2 * ny
+    sizes = (nx, nz, ny, block, strip, tokens, rows_i)
+    half = nz // 2
+    bf16, f32 = jnp.bfloat16, jnp.float32
+    sem = pltpu.SemaphoreType.DMA
+    square = (block, block)
+    return pl.pallas_call(
+        functools.partial(gather_kernel, sizes),
+        out_shape=(
+            jax.ShapeDtypeStruct((nx, rows_i, strip, block), f32),
+            jax.ShapeDtypeStruct((4, block, block), f32),
+        ),
+        in_specs=[pl.BlockSpec(memory_space=pl.ANY)] * 4,
+        out_specs=(pl.BlockSpec(memory_space=pltpu.VMEM),) * 2,
+        scratch_shapes=[
+            pltpu.VMEM((nz, nx, tokens, block), bf16),
+            pltpu.VMEM((nz, nx, rows_i, rows_z, tokens), bf16),
+            pltpu.VMEM((rows_i, rows_z, block), f32),
+            pltpu.VMEM((4, block, block), f32),
+            pltpu.VMEM(square, f32),
+        ]
+        + [pltpu.VMEM(square, bf16)] * 6
+        + [
+            sem((2,)), sem((4,)),
+            sem((nx - 1,)), sem((nx - 1,)),
+            sem((nz - 1,)), sem((nz - 1,)),
+            sem((2, half, nx)), sem((2, half, nx)),
+            sem((nx - 1,)), sem((nx - 1,)),
+            sem((nx, ny - 1)), sem((nx, ny - 1)),
+            sem((nx, ny)), sem((nx, ny)),
+            sem((nx - 1,)), sem((nx - 1,)),
+        ],
+        compiler_params=pltpu.CompilerParams(
+            collective_id=0, has_side_effects=True, vmem_limit_bytes=48 * 1024 * 1024
+        ),
+    )(act, cot, stats_left, stats_right)
 
 
 def product(left, right):
     return jnp.einsum("...ij,...jk->...ik", left, right, precision=HIGH)
-
-
-def root_of(statistic):
-    order = statistic.shape[-1]
-    identity = jnp.eye(order, dtype=jnp.float32)
-    bound = jnp.max(jnp.sum(jnp.abs(statistic), axis=-1), axis=-1)
-    factor = 1.25 * identity - statistic * (0.25 / bound)[..., None, None]
-    square = product(factor, factor)
-    cubic = product(square, 4.0 * square - 5.0 * factor)
-    return 1.25 * factor + 0.25 * product(square, cubic)
 
 
 def slot_targets(owner_ids, capacity):
@@ -31,9 +328,7 @@
 
 def per_device(activations, cotangents, owners, stats_left, stats_right, variance):
     tokens, block = activations.shape
-    columns = cotangents.shape[1] // block
     count = owners.shape[0]
-    rows = count // columns
     capacity = stats_left.shape[2]
     devices = X * Z
     strip = block // devices
@@ -42,23 +337,10 @@
     slot_ids = jnp.arange(devices * capacity, dtype=jnp.int32)
     select = targets[:, None] == slot_ids[None, :]
 
-    left_root = root_of(stats_left[0, 0])
-    right_root = root_of(stats_right[0, 0])
-
-    cot = cotangents.reshape(tokens, columns, block).transpose(1, 0, 2)
-    cot = lax.all_to_all(cot, "x", 0, 0, tiled=True)
-    cot = lax.all_gather(cot.reshape(X * tokens, block), "z", axis=0, tiled=True)
-
     act = activations.T.reshape(X, Z, strip, tokens).transpose(1, 0, 2, 3)
-    act = lax.all_to_all(act, "z", 0, 0, tiled=True)
     act = act.reshape(Z, X * strip, tokens)
-    act = lax.all_gather(act, ("x", "y", "c"), axis=0, tiled=False)
-    act = act.reshape(X, rows, Z, X * strip, tokens)
-    cot = cot.reshape(Z, X, tokens, block)
-    grad = jnp.einsum("xizrt,zxtc->irc", act, cot, preferred_element_type=jnp.float32)
-
-    grad = grad.reshape(rows, X, strip, block).transpose(1, 0, 2, 3)
-    grad = lax.all_to_all(grad, "x", 0, 0, tiled=True)
+    grad, roots = gather_and_roots(act, cotangents, stats_left[0, 0], stats_right[0, 0])
+    left_root, right_root = roots[:2], roots[2:]
     grad = grad.transpose(2, 1, 0, 3).reshape(strip, count, block)
 
     var_new = 0.9 * variance[0] + 0.1 * grad * grad

time: 269 us -> 174 us (0.65)
  waiting for transfers between devices: 131 us -> 53 us
  Pallas kernels: 0 us -> 68.9 us
  blocking collectives: 31.1 us -> 0 us
  matrix products: 44.8 us -> 14.9 us
  between operations: 14.3 us -> 0.8 us
  starting transfers between devices: 22.3 us -> 15.5 us
  other arithmetic: 11.1 us -> 4.46 us
    all_gather x2 -> x0, waiting for transfers between devices: 87.6 us -> none  [the longest x1 51.8 us: per_device(): act = lax.all_gather(act, ('x', 'y', 'c'), axis=0, tiled=False)]
    pallas_call x0 -> x1, Pallas kernels: none -> 68.9 us  [gather_and_roots(): pl.pallas_call(functools.partial(gather_kernel, sizes), out_shape=(jax.Sh...]
    all_to_all x2 -> x0, blocking collectives: 31.1 us -> none  [the longest x1 17.6 us: per_device(): act = lax.all_to_all(act, 'z', 0, 0, tiled=True)]
    dot_general x10 -> x4, matrix products: 33.1 us -> 11.1 us  [product(): return jnp.einsum('...ij,...jk->...ik', left, right, precision=HIGH)]
    all_to_all x1, waiting for transfers between devices: 13.5 us -> 27.1 us  [per_device(): coded = lax.all_to_all(coded, ('x', 'z'), 0, 0, tiled=True)]
    all_to_all x1 -> x0, waiting for transfers between devices: 6.86 us -> none  [per_device(): grad = lax.all_to_all(grad, 'x', 0, 0, tiled=True)]
    unnamed x31 -> x22, local copies, waits for them, and re-layouts: 6.71 us -> 12.2 us
    dot_general x1 -> x0, matrix products: 5.44 us -> none  [per_device(): jnp.einsum('xizrt,zxtc->irc', act, cot, preferred_element_type=jnp.float32)]
  transfers between devices with their start and end apart: 6 -> 3, of which waited for: 6 -> 3; matrix products, arithmetic and copies ran while one was open for 14% -> 7% of each run, Pallas kernels for 0% -> 0%
where the time goes in v2:
time: 174 us; the launch traced here: 173 us
  Pallas kernels  68.9 us (40%)
  waiting for transfers between devices  53 us (30%)
  local copies, waits for them, and re-layouts  15.5 us (9%)
  starting transfers between devices  15.5 us (9%)
  matrix products  14.9 us (9%)
  other arithmetic  4.46 us (3%)
    pallas_call x1, Pallas kernels, gather_and_roots(): pl.pallas_call(functools.partial(gather_kernel, sizes), out_shape=(jax.Sh...  68.9 us
    all_to_all x1, waiting for transfers between devices, per_device(): coded = lax.all_to_all(coded, ('x', 'z'), 0, 0, tiled=True)  27.1 us
    all_to_all x1, waiting for transfers between devices, per_device(): finished = lax.all_to_all(finished, ('x', 'z'), 0, 0, tiled=True)  17.8 us
    unnamed x22, local copies, waits for them, and re-layouts  12.2 us
    dot_general x4, matrix products, product(): return jnp.einsum('...ij,...jk->...ik', left, right, precision=HIGH)  11.1 us
    all_to_all x1, waiting for transfers between devices, per_device(): extra = lax.all_to_all(extra, ('x', 'z'), 0, 0, tiled=True)  7.99 us
    all_to_all x1, starting transfers between devices, per_device(): extra = lax.all_to_all(extra, ('x', 'z'), 0, 0, tiled=True)  6.29 us
    all_to_all x1, starting transfers between devices, per_device(): finished = lax.all_to_all(finished, ('x', 'z'), 0, 0, tiled=True)  5.13 us
  transfers between devices with their start and end apart: 3, of which 3 were waited for; matrix products, arithmetic and copies ran while one was open for 7% of the time, Pallas kernels for 0%

profile of v2, /device:TPU:8, one launch (start us, length us, event | category | flops | bytes accessed | tf_op | source)
XLA Modules:
  0.0 173.1 jit_solution(2919677683949697891)
XLA Ops:
  0.6 1.0 copy.62
  1.7 0.0 copy-start
  1.7 1.6 copy-done
  3.3 0.0 copy-start.2
  3.3 1.6 copy-done.2
  4.9 0.0 copy-start.4
  4.9 1.0 copy-done.4
  5.9 68.9 %shard_map.93 = (f32[4,8,16,512]{3,2,1,0:T(8,128)S(1)}, f32[4,512,512]{2,1,0:T(8,128)}) custom-call(bf16[8,64,128]{2,1,0:T(8,128)(2,1)S(1)} %bitcast.59, bf16[128,2048]{1,0:T(8,128)(2,1)S(1)} %copy-done.4, f32[2,512,512]{2,1,0:T(8,128)S(1)} %bitcast.57, f32[2,512,512]{2,1,0:T(8,128)S(1)} %bitcast.56), custom_call_target="tpu_custom_call" | custom-call | tf_op jit(solution)/shard_map/pallas_call | solution.py:285
  74.8 0.0 copy-start.8
  74.8 0.1 copy.64
  74.9 1.1 copy-done.8
  76.1 1.8 %fusion.5 = (f32[1,16,32,512]{3,1,2,0:T(8,128)}, f32[1,16,32,512]{3,1,2,0:T(8,128)S(1)}) fusion(f32[16,8,4,512]{3,0,2,1:T(8,128)S(1)} %copy.64, f32[1,16,32,512]{3,2,1,0:T(8,128)S(1)} %copy-done.8), kind=kLoop, calls=%fused_computation.15 | loop fusion | flops 1048576 | bytes 4194304 | tf_op jit(solution)/shard_map/add | solution.py:346
  77.8 0.0 copy-start.9
  77.8 0.4 fusion.9
  78.2 0.1 copy.70
  78.3 0.1 broadcast_in_dim.16
  78.4 0.1 copy-done.9
  78.5 0.2 convert_reduce_fusion
  78.7 0.1 select_reduce_fusion
  78.8 0.2 concatenate.8
  78.9 1.7 %abs_reduce_fusion = (f32[64,16]{0,1:T(8,128)S(1)}, f32[64,16,512]{2,0,1:T(8,128)S(1)}) fusion(f32[16,32,512]{2,0,1:T(8,128)S(1)} %bitcast.63, s32[32]{0:T(128)S(1)} %fusion.16), kind=kOutput, calls=%fused_computation.9 | convolution fusion | flops 202376192 | bytes 3149952 | tf_op jit(solution)/shard_map/rbc,bq->qrc/dot_general | solution.py:349
  80.7 0.1 copy.67
  80.8 0.7 pad_maximum_fusion
  81.5 6.3 %all-to-all-start.1 = ((f32[32,2,17]{2,1,0:T(2,128)}), f32[32,2,17]{2,1,0:T(2,128)S(1)}, u32[]{:S(2)}, u32[]{:S(2)}) async-start(f32[32,2,17]{2,1,0:T(2,128)} %pad_maximum_fusion), calls=%async_computation.1 | async-start | bytes 65536 | tf_op jit(solution)/shard_map/all_to_all | solution.py:358
  87.8 0.4 round-nearest-even_convert_fusion
  88.2 1.5 copy.66
  89.7 8.0 %all-to-all-done.1 = f32[32,2,17]{2,1,0:T(2,128)S(1)} async-done(((f32[32,2,17]{2,1,0:T(2,128)}), f32[32,2,17]{2,1,0:T(2,128)S(1)}, u32[]{:S(2)}, u32[]{:S(2)}) %all-to-all-start.1) | async-done | bytes 4384 | tf_op jit(solution)/shard_map/all_to_all | solution.py:358
  97.7 4.1 %all-to-all-start = ((s16[64,16,512]{2,1,0:T(8,128)(2,1)}), s16[64,16,512]{2,1,0:T(8,128)(2,1)S(1)}, u32[]{:S(2)}, u32[]{:S(2)}) async-start(s16[64,16,512]{2,1,0:T(8,128)(2,1)} %copy.66), calls=%async_computation | async-start | bytes 2097152 | tf_op jit(solution)/shard_map/all_to_all | solution.py:357
  101.8 0.2 slice_reduce_fusion
  102.1 27.1 %all-to-all-done = s16[64,16,512]{2,1,0:T(8,128)(2,1)S(1)} async-done(((s16[64,16,512]{2,1,0:T(8,128)(2,1)}), s16[64,16,512]{2,1,0:T(8,128)(2,1)S(1)}, u32[]{:S(2)}, u32[]{:S(2)}) %all-to-all-start) | async-done | bytes 1048608 | tf_op jit(solution)/shard_map/all_to_all | solution.py:357
  129.2 0.4 fusion
  129.6 0.0 copy-start.7
  129.6 0.2 copy.72
  129.8 0.0 copy-start.5
  129.8 1.3 copy-done.5
  131.1 1.4 copy-done.7
  132.5 2.1 %fusion.18 = f32[2,512,512]{2,1,0:T(8,128)S(1)} fusion(f32[4,512,512]{2,1,0:T(8,128)S(1)} %copy-done.7, f32[2,512,512]{2,1,0:T(8,128)S(1)} %bitcast.60), kind=kOutput, calls=%fused_computation.39 | convolution fusion | flops 1610612736 | bytes 8388608 | tf_op jit(solution)/shard_map/...ij,...jk->...ik/dot_general | solution.py:318
  134.6 2.2 %multiply_reduce_fusion = (f32[2]{0:T(128)S(1)}, f32[2,512,512]{2,1,0:T(8,128)S(1)}) fusion(f32[2,512,512]{2,1,0:T(8,128)S(1)} %fusion.18, f32[4,512,512]{2,1,0:T(8,128)S(1)} %copy-done.7), kind=kOutput, calls=%fused_computation.5 | convolution fusion | flops 1611661312 | bytes 6291464 | tf_op jit(solution)/shard_map/...ij,...jk->...ik/dot_general | solution.py:318
  136.8 0.3 multiply_convert_fusion
  137.2 1.0 copy.93
  138.2 0.0 copy-start.1
  138.2 5.1 %all-to-all-start.2 = ((bf16[32,2,16,512]{3,2,1,0:T(8,128)(2,1)}), bf16[32,2,16,512]{3,2,1,0:T(8,128)(2,1)S(1)}, u32[]{:S(2)}, u32[]{:S(2)}) async-start(bf16[32,2,16,512]{3,2,1,0:T(8,128)(2,1)} %bitcast.66), calls=%async_computation.2 | async-start | bytes 2097152 | tf_op jit(solution)/shard_map/all_to_all | solution.py:371
  143.3 0.0 copy-start.6
  143.3 3.0 %copy.77 = f32[1,16,32,512]{3,2,1,0:T(8,128)} copy(f32[1,16,32,512]{3,1,2,0:T(8,128)} %get-tuple-element.24) | data formatting | bytes 2097152
  146.3 0.0 copy-done.1
  146.3 0.0 copy-done.6
  146.3 0.0 copy-start.3
  146.3 3.4 %bitcast_add_fusion = f32[1,1,2,512,512]{4,3,2,1,0:T(8,128)} fusion(f32[1,1,2,512,512]{4,3,2,1,0:T(8,128)S(1)} %copy-done.1, f32[2,512,512]{2,1,0:T(8,128)S(1)} %bitcast.61), kind=kOutput, calls=%fused_computation.2 | convolution fusion | flops 1612185600 | bytes 6291456 | tf_op jit(solution)/shard_map/...ij,...jk->...ik/dot_general | solution.py:318
  149.7 0.0 copy-done.3
  149.7 3.4 %bitcast_add_fusion.1 = f32[1,1,2,512,512]{4,3,2,1,0:T(8,128)} fusion(f32[1,1,2,512,512]{4,3,2,1,0:T(8,128)S(1)} %copy-done.3, f32[2,512,512]{2,1,0:T(8,128)S(1)} %bitcast.62), kind=kOutput, calls=%fused_computation.3 | convolution fusion | flops 1612185600 | bytes 6291456 | tf_op jit(solution)/shard_map/...ij,...jk->...ik/dot_general | solution.py:318
  153.1 17.8 %all-to-all-done.2 = bf16[32,2,16,512]{3,2,1,0:T(8,128)(2,1)S(1)} async-done(((bf16[32,2,16,512]{3,2,1,0:T(8,128)(2,1)}), bf16[32,2,16,512]{3,2,1,0:T(8,128)(2,1)S(1)}, u32[]{:S(2)}, u32[]{:S(2)}) %all-to-all-start.2) | async-done | bytes 1048608 | tf_op jit(solution)/shard_map/all_to_all | solution.py:371
  171.0 2.1 %convolution_bitcast_fusion = bf16[1,16,32,512]{3,2,1,0:T(8,128)(2,1)} fusion(bf16[64,16,512]{2,1,0:T(8,128)(2,1)S(1)} %bitcast.65, s32[32]{0:T(128)S(1)} %fusion.16), kind=kOutput, calls=%fused_computation.12 | convolution fusion | flops 33556480 | bytes 1572992 | tf_op jit(solution)/shard_map/qrc,bq->rbc/dot_general | solution.py:373
  (5 shorter events, 0.1 us)
Async XLA Ops:
  1.7 1.6 copy-start
  3.3 1.6 copy-start.2
  4.9 1.0 copy-start.4
  74.8 1.2 copy-start.8
  77.8 0.7 copy-start.9
  81.5 16.2 %all-to-all-start.1 = ((f32[32,2,17]{2,1,0:T(2,128)}), f32[32,2,17]{2,1,0:T(2,128)S(1)}, u32[]{:S(2)}, u32[]{:S(2)}) async-start(f32[32,2,17]{2,1,0:T(2,128)} %pad_maximum_fusion), calls=%async_computation.1 | async-start | bytes 65536 | tf_op jit(solution)/shard_map/all_to_all | solution.py:358
  97.7 31.5 %all-to-all-start = ((s16[64,16,512]{2,1,0:T(8,128)(2,1)}), s16[64,16,512]{2,1,0:T(8,128)(2,1)S(1)}, u32[]{:S(2)}, u32[]{:S(2)}) async-start(s16[64,16,512]{2,1,0:T(8,128)(2,1)} %copy.66), calls=%async_computation | async-start | bytes 2097152 | tf_op jit(solution)/shard_map/all_to_all | solution.py:357
  129.6 2.9 %copy-start.7 = (f32[4,512,512]{2,1,0:T(8,128)S(1)}, f32[4,512,512]{2,1,0:T(8,128)}, u32[]{:S(2)}) copy-start(f32[4,512,512]{2,1,0:T(8,128)} %get-tuple-element.6) | copy-start | bytes 12582916
  129.8 1.3 copy-start.5
  138.2 8.1 %copy-start.1 = (f32[1,1,2,512,512]{4,3,2,1,0:T(8,128)S(1)}, f32[1,1,2,512,512]{4,3,2,1,0:T(8,128)}, u32[]{:S(2)}) copy-start(f32[1,1,2,512,512]{4,3,2,1,0:T(8,128)} %param.10) | copy-start | bytes 6291460
  138.2 32.8 %all-to-all-start.2 = ((bf16[32,2,16,512]{3,2,1,0:T(8,128)(2,1)}), bf16[32,2,16,512]{3,2,1,0:T(8,128)(2,1)S(1)}, u32[]{:S(2)}, u32[]{:S(2)}) async-start(bf16[32,2,16,512]{3,2,1,0:T(8,128)(2,1)} %bitcast.66), calls=%async_computation.2 | async-start | bytes 2097152 | tf_op jit(solution)/shard_map/all_to_all | solution.py:371
  143.3 3.0 %copy-start.6 = (f32[2,32,16,512]{3,2,1,0:T(8,128)S(1)}, f32[2,32,16,512]{3,2,1,0:T(8,128)}, u32[]{:S(2)}) copy-start(f32[2,32,16,512]{3,2,1,0:T(8,128)} %copy-done.5) | copy-start | bytes 6291460
  146.3 3.4 %copy-start.3 = (f32[1,1,2,512,512]{4,3,2,1,0:T(8,128)S(1)}, f32[1,1,2,512,512]{4,3,2,1,0:T(8,128)}, u32[]{:S(2)}) copy-start(f32[1,1,2,512,512]{4,3,2,1,0:T(8,128)} %param.9) | copy-start | bytes 6291460

commit v3 on v2

--- a/solution.py
+++ b/solution.py
@@ -8,7 +8,6 @@
 from jax.sharding import Mesh, PartitionSpec as P
 
 X, Z, Y = 4, 8, 4
-HIGH = lax.Precision.HIGH
 MESH = pl.DeviceIdType.MESH
 COEFFICIENTS = (
     25 / 16, -5 / 16 - 3125 / 4096, 3125 / 4096, -1250 / 4096, 250 / 4096, -25 / 4096, 1 / 4096,
@@ -37,17 +36,23 @@
     lax.fori_loop(0, 2, one, 0)
 
 
-def gather_kernel(
-    sizes, act, cot, stats_left, stats_right, strips, roots,
-    cbuf, abuf, grad, sbuf, m2, m_h, m_l, m2_h, m2_l, w_h, w_l,
-    own_sem, stat_sem, c1_s, c1_r, a1_s, a1_r, zr_s, zr_r, a2_s, a2_r,
-    y_s, y_r, sib_s, sib_r, ex_s, ex_r,
+def step_kernel(
+    sizes, act, cot, stats_left, stats_right, variance, source, targets, used,
+    direction, left_new, right_new, var_new,
+    cbuf, abuf, grad, sbuf, vbuf, vt, matrix, m2, m_h, m_l, m2_h, m2_l, w_h, w_l, root_h, root_l,
+    gsend, gsend_row, gq, gq_row, scale_rows, adam_rows, send_q, send_row, rq, rq_row,
+    owned_h, owned_l, pre, finished, ret,
+    own_sem, stat_sem, out_sem, var_sem, c1_s, c1_r, a1_s, a1_r, zr_s, zr_r, a2_s, a2_r,
+    y_s, y_r, sib_s, sib_r, ex_s, ex_r, exr_s, exr_r, go_s, go_r, gor_s, gor_r, back_s, back_r,
 ):
     nx, nz, ny, block, strip, tokens, rows_i = sizes
+    count, devices, width = rows_i * nx, nx * nz, rows_i * strip
+    lane = vbuf.shape[2]
     half = nz // 2
     x, z = lax.axis_index("x"), lax.axis_index("z")
     y, c = lax.axis_index("y"), lax.axis_index("c")
     mine = 2 * y + c
+    me = x * nz + z
 
     def remote(src, dst, send, recv, **where):
         return pltpu.make_async_remote_copy(
@@ -64,19 +69,33 @@
         cot.at[:, pl.ds(pl.multiple_of(x * block, block), block)], cbuf.at[z, x], own_sem.at[0]
     )
     own_a = pltpu.make_async_copy(act.at[z], abuf.at[z, x, mine], own_sem.at[1])
+    loads += [
+        pltpu.make_async_copy(
+            variance.at[:, k * lane : (k + 1) * lane], vbuf.at[k], var_sem.at[0, k]
+        )
+        for k in range(block // lane)
+    ]
     own_c.start()
     own_a.start()
     for load in loads:
         load.start()
 
     barrier = pltpu.get_barrier_semaphore()
-    partners = [{"x": lax.rem(x + d, nx)} for d in range(1, nx)]
-    partners += [{"z": lax.rem(z + d, nz)} for d in range(1, nz)]
-    partners += [{"y": lax.rem(y + d, ny)} for d in range(1, ny)]
+
+    def plane(d):
+        return lax.rem(x + d // nz, nx), lax.rem(z + lax.rem(d, nz), nz)
+
+    def greet(d, carry):
+        x2, z2 = plane(d)
+        pl.semaphore_signal(barrier, inc=1, device_id={"x": x2, "z": z2}, device_id_type=MESH)
+        return carry
+
+    lax.fori_loop(1, devices, greet, 0)
+    partners = [{"y": lax.rem(y + d, ny)} for d in range(1, ny)]
     partners += [{"c": 1 - c}]
     for partner in partners:
         pl.semaphore_signal(barrier, inc=1, device_id=partner, device_id_type=MESH)
-    pl.semaphore_wait(barrier, len(partners))
+    pl.semaphore_wait(barrier, len(partners) + devices - 1)
 
     sends = []
 
@@ -180,34 +199,45 @@
             if t == 0:
                 stat = sbuf[q]
                 bound = jnp.max(jnp.sum(jnp.abs(stat), axis=1, keepdims=True), axis=0, keepdims=True)
-                matrix = stat * (1.0 / bound)
-                sbuf[q] = matrix
-                m_h[...], m_l[...] = halves(matrix)
+                value = stat * (1.0 / bound)
+                matrix[...] = value
+                m_h[...], m_l[...] = halves(value)
 
                 def finish(rows, value):
                     m2[rows, :] = value
                     m2_h[rows, :], m2_l[rows, :] = halves(value)
                     w_h[rows, :], w_l[rows, :] = halves(
-                        COEFFICIENTS[5] * sbuf[q, rows, :] + COEFFICIENTS[6] * value
+                        COEFFICIENTS[5] * matrix[rows, :] + COEFFICIENTS[6] * value
                     )
 
                 tiled_product(m_h, m_l, m_h, m_l, block, finish)
             elif t == 1:
 
                 def finish(rows, value):
-                    value += COEFFICIENTS[3] * sbuf[q, rows, :] + COEFFICIENTS[4] * m2[rows, :]
+                    value += COEFFICIENTS[3] * matrix[rows, :] + COEFFICIENTS[4] * m2[rows, :]
                     m_h[rows, :], m_l[rows, :] = halves(value)
 
                 tiled_product(m2_h, m2_l, w_h, w_l, block, finish)
             else:
 
                 def finish(rows, value):
-                    value += COEFFICIENTS[1] * sbuf[q, rows, :] + COEFFICIENTS[2] * m2[rows, :]
+                    value += COEFFICIENTS[1] * matrix[rows, :] + COEFFICIENTS[2] * m2[rows, :]
                     ids = lax.broadcasted_iota(jnp.int32, value.shape, 0) + rows.start
                     columns = lax.broadcasted_iota(jnp.int32, value.shape, 1)
-                    roots[q, rows, :] = value + jnp.where(ids == columns, COEFFICIENTS[0], 0.0)
+                    value += jnp.where(ids == columns, COEFFICIENTS[0], 0.0)
+                    root_h[q, rows, :], root_l[q, rows, :] = halves(value)
 
                 tiled_product(m2_h, m2_l, m_h, m_l, block, finish)
+
+            each = -(-count // 12)
+            for extra in range(each):
+                b = n * each + extra
+
+                @pl.when(b < count)
+                def _():
+                    rows = pl.ds(pl.multiple_of(b * strip, strip), strip)
+                    for k in range(block // lane):
+                        vt[k, rows, :] = vbuf[k, pl.ds(b, strip, stride=count), :]
         return carry
 
     lax.fori_loop(0, 4, one_matrix, 0)
@@ -241,20 +271,214 @@
 
     def exchange(d):
         j = lax.rem(x + d, nx)
+        return (
+            remote(gsend.at[j], gq.at[x], ex_s.at[d - 1], ex_r.at[d - 1], x=j),
+            remote(gsend_row.at[j], gq_row.at[x], exr_s.at[d - 1], exr_r.at[d - 1], x=j),
+        )
+
+    diagonal = lax.broadcasted_iota(jnp.int32, (width, width), 0) == lax.broadcasted_iota(
+        jnp.int32, (width, width), 1
+    )
+    for d in list(range(1, nx)) + [0]:
+        j = lax.rem(x + d, nx)
         rows = pl.ds(pl.multiple_of(j * strip, strip), strip)
-        return rows, remote(
-            grad.at[:, rows, :], strips.at[x], ex_s.at[d - 1], ex_r.at[d - 1], x=j
-        )
-
+        value = grad[:, rows, :].reshape(width, block) + shard(far, rows)
+        top = jnp.maximum(jnp.max(jnp.abs(value), axis=1, keepdims=True), 1e-30)
+        coded = jnp.round(value * (32767.0 / top)).astype(jnp.int32).astype(jnp.int16)
+        row = jnp.sum(jnp.where(diagonal, top * (1.0 / 32767.0), 0.0), axis=0, keepdims=True)
+        if d:
+            gsend[j] = coded.reshape(rows_i, strip, block)
+            gsend_row[j] = row
+            for copy in exchange(d):
+                launch(copy)
+        else:
+            gq[x] = coded.reshape(rows_i, strip, block)
+            gq_row[x] = row
+
+    lanes = lax.broadcasted_iota(jnp.int32, (1, width), 1)
+
+    def strips_of(j):
+        row = gq_row[j]
+        column = jnp.sum(jnp.where(diagonal, row, 0.0), axis=1, keepdims=True)
+        for i in range(rows_i):
+            b = i * nx + j
+            value = gq[j, i].astype(jnp.float32) * column[i * strip : (i + 1) * strip]
+            square = value * value
+            rows = pl.ds(pl.multiple_of(b * strip, strip), strip)
+            old = jnp.concatenate([vt[k, rows, :] for k in range(block // lane)], axis=1)
+            fresh = 0.9 * old + 0.1 * square
+            for k in range(block // lane):
+                vt[k, rows, :] = fresh[:, k * lane : (k + 1) * lane]
+            total = jnp.sum(square / fresh, axis=0, keepdims=True)
+            adam_rows[pl.ds(b, 1), :] = sum(
+                total[:, k * width : (k + 1) * width] for k in range(block // width)
+            )
+            inside = jnp.logical_and(lanes >= i * strip, lanes < (i + 1) * strip)
+            scale_rows[pl.ds(b, 1), :] = jnp.where(inside, row, 0.0)
+
+    strips_of(x)
     for d in range(1, nx):
-        rows, copy = exchange(d)
-        grad[:, rows, :] += shard(far, rows).reshape(rows_i, strip, block)
-        launch(copy)
-    rows = pl.ds(pl.multiple_of(x * strip, strip), strip)
-    strips[x] = grad[:, rows, :] + shard(far, rows).reshape(rows_i, strip, block)
-    for d in range(1, nx):
-        exchange(d)[1].wait_recv()
-
+        for copy in exchange(d):
+            copy.wait_recv()
+        strips_of(lax.rem(x - d + nx, nx))
+
+    def go(slot, d):
+        x2, z2 = plane(d)
+        other = x2 * nz + z2
+        return (
+            remote(send_q.at[slot, other], rq.at[slot, me],
+                   go_s.at[slot, d - 1], go_r.at[slot, d - 1], x=x2, z=z2),
+            remote(send_row.at[slot, other], rq_row.at[slot, me],
+                   gor_s.at[slot, d - 1], gor_r.at[slot, d - 1], x=x2, z=z2),
+        )
+
+    def picked(slot, other):
+        b = source[2 * other + slot]
+        rows = jnp.concatenate([scale_rows[pl.ds(b, 1), :], adam_rows[pl.ds(b, 1), :]], axis=0)
+        return gq[lax.rem(b, nx), b // nx], rows
+
+    for slot in range(2):
+
+        def send(d, carry):
+            x2, z2 = plane(d)
+            other = x2 * nz + z2
+            send_q[slot, other], send_row[slot, other] = picked(slot, other)
+            for copy in go(slot, d):
+                copy.start()
+            return carry
+
+        lax.fori_loop(1, devices, send, 0)
+        rq[slot, me], rq_row[slot, me] = picked(slot, me)
+
+    def reorder(r, carry):
+        rows = pl.ds(pl.multiple_of(r * count, count), count)
+        for k in range(block // lane):
+            vbuf[k, rows, :] = vt[k, pl.ds(r, count, stride=strip), :]
+        return carry
+
+    lax.fori_loop(0, strip, reorder, 0)
+    outs = [
+        pltpu.make_async_copy(
+            vbuf.at[k], var_new.at[:, k * lane : (k + 1) * lane], var_sem.at[1, k]
+        )
+        for k in range(block // lane)
+    ]
+    for copy in outs:
+        copy.start()
+
+    def arrival(d):
+        return lax.rem(x - d // nz + nx, nx) * nz + lax.rem(z - lax.rem(d, nz) + nz, nz)
+
+    def back(slot, d):
+        x2, z2 = plane(d)
+        other = x2 * nz + z2
+        rows = pl.ds(pl.multiple_of(other * strip, strip), strip)
+        return remote(
+            finished.at[slot, rows, :], ret.at[2 * me + slot],
+            back_s.at[slot, d - 1], back_r.at[slot, d - 1], x=x2, z=z2,
+        )
+
+    fits = lax.rem(lax.broadcasted_iota(jnp.int32, (strip, width), 1), strip) == (
+        lax.broadcasted_iota(jnp.int32, (strip, width), 0)
+    )
+    for slot in range(2):
+        keep = used[slot]
+
+        def decode(p, total):
+            extra = rq_row[slot, p]
+            column = jnp.sum(jnp.where(fits, extra[0:1], 0.0), axis=1, keepdims=True) * keep
+            value = rq[slot, p].astype(jnp.float32) * column
+            rows = pl.ds(pl.multiple_of(p * strip, strip), strip)
+            owned_h[slot, rows, :], owned_l[slot, rows, :] = halves(value)
+            return total + extra[1:2]
+
+        def receive(d, total):
+            for copy in go(slot, d):
+                copy.wait_recv()
+            return decode(arrival(d), total)
+
+        total = decode(me, jnp.zeros((1, width), jnp.float32))
+        total = lax.fori_loop(1, devices, receive, total)
+
+        def finish(rows, value):
+            m_h[rows, :], m_l[rows, :] = halves(value)
+
+        tiled_product(
+            root_h.at[slot], root_l.at[slot], owned_h.at[slot], owned_l.at[slot], block, finish
+        )
+
+        def finish(rows, value):
+            pre[rows, :] = value
+
+        tiled_product(m_h, m_l, root_h.at[2 + slot], root_l.at[2 + slot], block, finish)
+        value = pre[...]
+        squares = jnp.sum(jnp.sum(value * value, axis=0, keepdims=True), axis=1, keepdims=True)
+        mean_adam = jnp.sum(total, axis=1, keepdims=True) * (1.0 / (block * block))
+        ratio = jnp.sqrt(mean_adam / (squares * (1.0 / (block * block)) + 1e-6))
+        finished[slot] = (value * ratio).astype(jnp.bfloat16)
+
+        def send_back(d, carry):
+            back(slot, d).start()
+            return carry
+
+        lax.fori_loop(1, devices, send_back, 0)
+        rows = pl.ds(pl.multiple_of(me * strip, strip), strip)
+        ret[2 * me + slot] = finished[slot, rows, :]
+
+    tile = block // 2
+    for slot in range(2):
+
+        def outer(step, carry):
+            rows = pl.ds(pl.multiple_of(step * tile, tile), tile)
+
+            def pair(dims, left_high, left_low):
+                def one(left, right):
+                    return lax.dot_general(
+                        left, right, (dims, ((), ())), preferred_element_type=jnp.float32
+                    )
+
+                total = one(left_high, owned_l[slot]) + one(left_low, owned_h[slot])
+                return one(left_high, owned_h[slot]) + total
+
+            left = pair(((1,), (1,)), owned_h[slot, rows, :], owned_l[slot, rows, :])
+            sbuf[slot, rows, :] = 0.9 * sbuf[slot, rows, :] + 0.1 * left
+            right = pair(((0,), (0,)), owned_h[slot, :, rows], owned_l[slot, :, rows])
+            sbuf[2 + slot, rows, :] = 0.9 * sbuf[2 + slot, rows, :] + 0.1 * right
+            return carry
+
+        lax.fori_loop(0, 2, outer, 0)
+        outs.append(pltpu.make_async_copy(sbuf.at[slot], left_new.at[slot], out_sem.at[slot]))
+        outs.append(
+            pltpu.make_async_copy(sbuf.at[2 + slot], right_new.at[slot], out_sem.at[2 + slot])
+        )
+        for copy in outs[-2:]:
+            copy.start()
+
+    for slot in range(2):
+
+        def collect(d, carry):
+            back(slot, d).wait_recv()
+            return carry
+
+        lax.fori_loop(1, devices, collect, 0)
+
+    def choose(b, carry):
+        direction[b] = ret[targets[b]]
+        return carry
+
+    lax.fori_loop(0, count, choose, 0)
+
+    for copy in outs:
+        copy.wait()
+    for slot in range(2):
+
+        def drain(d, carry):
+            for copy in go(slot, d):
+                copy.wait_send()
+            back(slot, d).wait_send()
+            return carry
+
+        lax.fori_loop(1, devices, drain, 0)
     for copy in sends:
         copy.wait_send()
     for hop in range(1, half):
@@ -271,7 +495,7 @@
                 sibling(k, d).wait_send()
 
 
-def gather_and_roots(act, cot, stats_left, stats_right):
+def shampoo(act, cot, stats_left, stats_right, variance, source, targets, used):
     nz, rows_z, tokens = act.shape
     nx, ny = lax.axis_size("x"), lax.axis_size("y")
     block = stats_left.shape[-1]
@@ -279,43 +503,66 @@
     rows_i = 2 * ny
     sizes = (nx, nz, ny, block, strip, tokens, rows_i)
     half = nz // 2
-    bf16, f32 = jnp.bfloat16, jnp.float32
-    sem = pltpu.SemaphoreType.DMA
+    count, devices, width = rows_i * nx, nx * nz, rows_i * strip
+    lane = min(block, 128)
+    bf16, f32, i16 = jnp.bfloat16, jnp.float32, jnp.int16
+    sem, vmem = pltpu.SemaphoreType.DMA, pltpu.VMEM
     square = (block, block)
+    anywhere = pl.BlockSpec(memory_space=pl.ANY)
+    scalars = pl.BlockSpec(memory_space=pltpu.SMEM)
     return pl.pallas_call(
-        functools.partial(gather_kernel, sizes),
+        functools.partial(step_kernel, sizes),
         out_shape=(
-            jax.ShapeDtypeStruct((nx, rows_i, strip, block), f32),
-            jax.ShapeDtypeStruct((4, block, block), f32),
+            jax.ShapeDtypeStruct((count, strip, block), bf16),
+            jax.ShapeDtypeStruct(stats_left.shape, f32),
+            jax.ShapeDtypeStruct(stats_right.shape, f32),
+            jax.ShapeDtypeStruct(variance.shape, f32),
         ),
-        in_specs=[pl.BlockSpec(memory_space=pl.ANY)] * 4,
-        out_specs=(pl.BlockSpec(memory_space=pltpu.VMEM),) * 2,
+        in_specs=[anywhere] * 5 + [scalars] * 3,
+        out_specs=(pl.BlockSpec(memory_space=pltpu.VMEM),) + (anywhere,) * 3,
         scratch_shapes=[
-            pltpu.VMEM((nz, nx, tokens, block), bf16),
-            pltpu.VMEM((nz, nx, rows_i, rows_z, tokens), bf16),
-            pltpu.VMEM((rows_i, rows_z, block), f32),
-            pltpu.VMEM((4, block, block), f32),
-            pltpu.VMEM(square, f32),
+            vmem((nz, nx, tokens, block), bf16),
+            vmem((nz, nx, rows_i, rows_z, tokens), bf16),
+            vmem((rows_i, rows_z, block), f32),
+            vmem((4, block, block), f32),
+            vmem((block // lane, strip * count, lane), f32),
+            vmem((block // lane, strip * count, lane), f32),
+            vmem(square, f32),
+            vmem(square, f32),
         ]
-        + [pltpu.VMEM(square, bf16)] * 6
+        + [vmem(square, bf16)] * 6
         + [
-            sem((2,)), sem((4,)),
+            vmem((4, block, block), bf16),
+            vmem((4, block, block), bf16),
+            vmem((nx, rows_i, strip, block), i16),
+            vmem((nx, 1, width), f32),
+            vmem((nx, rows_i, strip, block), i16),
+            vmem((nx, 1, width), f32),
+            vmem((count, width), f32),
+            vmem((count, width), f32),
+            vmem((2, devices, strip, block), i16),
+            vmem((2, devices, 2, width), f32),
+            vmem((2, devices, strip, block), i16),
+            vmem((2, devices, 2, width), f32),
+            vmem((2, block, block), bf16),
+            vmem((2, block, block), bf16),
+            vmem(square, f32),
+            vmem((2, block, block), bf16),
+            vmem((2 * devices, strip, block), bf16),
+            sem((2,)), sem((4,)), sem((4,)), sem((2, block // lane)),
             sem((nx - 1,)), sem((nx - 1,)),
             sem((nz - 1,)), sem((nz - 1,)),
             sem((2, half, nx)), sem((2, half, nx)),
             sem((nx - 1,)), sem((nx - 1,)),
-            sem((nx, ny - 1)), sem((nx, ny - 1)),
+            sem((nx, max(1, ny - 1))), sem((nx, max(1, ny - 1))),
             sem((nx, ny)), sem((nx, ny)),
-            sem((nx - 1,)), sem((nx - 1,)),
-        ],
+        ]
+        + [sem((nx - 1,))] * 4
+        + [sem((2, devices - 1))] * 6,
         compiler_params=pltpu.CompilerParams(
-            collective_id=0, has_side_effects=True, vmem_limit_bytes=48 * 1024 * 1024
+            collective_id=0, has_side_effects=True, vmem_limit_bytes=60 * 1024 * 1024
         ),
-    )(act, cot, stats_left, stats_right)
-
-
-def product(left, right):
-    return jnp.einsum("...ij,...jk->...ik", left, right, precision=HIGH)
+    )(act, cot, stats_left, stats_right, variance, source, targets, used)
 
 
 def slot_targets(owner_ids, capacity):
@@ -330,52 +577,26 @@
     tokens, block = activations.shape
     count = owners.shape[0]
     capacity = stats_left.shape[2]
-    devices = X * Z
+    devices = lax.axis_size("x") * lax.axis_size("z")
     strip = block // devices
 
     targets = slot_targets(owners[:, 0], capacity)
     slot_ids = jnp.arange(devices * capacity, dtype=jnp.int32)
     select = targets[:, None] == slot_ids[None, :]
-
-    act = activations.T.reshape(X, Z, strip, tokens).transpose(1, 0, 2, 3)
-    act = act.reshape(Z, X * strip, tokens)
-    grad, roots = gather_and_roots(act, cotangents, stats_left[0, 0], stats_right[0, 0])
-    left_root, right_root = roots[:2], roots[2:]
-    grad = grad.transpose(2, 1, 0, 3).reshape(strip, count, block)
-
-    var_new = 0.9 * variance[0] + 0.1 * grad * grad
-    sums_adam = jnp.sum(grad * grad / var_new, axis=(0, 2))
-
-    outgoing = jnp.einsum(
-        "rbc,bq->qrc", grad, select.astype(jnp.float32), precision=lax.Precision.HIGHEST
+    blocks = jnp.arange(count, dtype=jnp.int32)
+    source = jnp.sum(jnp.where(select, blocks[:, None], 0), axis=0)
+    me = lax.axis_index("x") * lax.axis_size("z") + lax.axis_index("z")
+    mine = me * capacity + jnp.arange(capacity, dtype=jnp.int32)
+    used = jnp.any(targets[:, None] == mine[None, :], axis=0).astype(jnp.float32)
+
+    act = activations.T.reshape(-1, lax.axis_size("z"), strip, tokens).transpose(1, 0, 2, 3)
+    act = act.reshape(lax.axis_size("z"), -1, tokens)
+    direction, left_new, right_new, var_new = shampoo(
+        act, cotangents, stats_left[0, 0], stats_right[0, 0],
+        variance.reshape(strip * count, block), source, targets, used,
     )
-    scale = jnp.maximum(jnp.max(jnp.abs(outgoing), axis=-1, keepdims=True), 1e-30)
-    coded = outgoing * (32767.0 / scale)
-    coded = jnp.round(coded).astype(jnp.int16)
-    sums_slot = jnp.sum(jnp.where(select, sums_adam[:, None], 0.0), axis=0)
-    extra = jnp.concatenate([scale[:, :, 0], sums_slot[:, None]], axis=1)
-    coded = lax.all_to_all(coded, ("x", "z"), 0, 0, tiled=True)
-    extra = lax.all_to_all(extra, ("x", "z"), 0, 0, tiled=True)
-    coded = coded.reshape(devices, capacity, strip, block).transpose(1, 0, 2, 3)
-    extra = extra.reshape(devices, capacity, strip + 1).transpose(1, 0, 2)
-    scale = extra[:, :, :strip] * (1.0 / 32767.0)
-    owned = coded.astype(jnp.float32) * scale[..., None]
-    owned = owned.reshape(capacity, block, block)
-
-    precond = product(product(left_root, owned), right_root)
-    mean_adam = jnp.sum(extra[:, :, strip], axis=1) / (block * block)
-    mean_pre = jnp.mean(precond * precond, axis=(1, 2))
-    ratio = jnp.sqrt(mean_adam / (mean_pre + 1e-6))
-    finished = (precond * ratio[:, None, None]).astype(jnp.bfloat16)
-    finished = finished.reshape(capacity, devices, strip, block).transpose(1, 0, 2, 3)
-    finished = lax.all_to_all(finished, ("x", "z"), 0, 0, tiled=True)
-    finished = finished.reshape(devices * capacity, strip, block)
-    direction = jnp.einsum("qrc,bq->rbc", finished, select.astype(jnp.bfloat16))
-
-    flipped = jnp.swapaxes(owned, -1, -2)
-    left_new = 0.9 * stats_left + 0.1 * product(owned, flipped)[None, None]
-    right_new = 0.9 * stats_right + 0.1 * product(flipped, owned)[None, None]
-    return (direction[None], left_new, right_new, var_new[None])
+    direction = direction.transpose(1, 0, 2)[None]
+    return (direction, left_new[None, None], right_new[None, None], var_new.reshape(variance.shape))
 
 
 def solution(mesh):

time: 174 us -> 133 us (0.76)
  waiting for transfers between devices: 53 us -> 0 us
  Pallas kernels: 68.9 us -> 118 us
  starting transfers between devices: 15.5 us -> 0 us
  matrix products: 14.9 us -> 0 us
  local copies, waits for them, and re-layouts: 15.5 us -> 9.98 us
    all_to_all x3 -> x0, waiting for transfers between devices: 53 us -> none  [the longest x1 27.1 us: per_device(): coded = lax.all_to_all(coded, ('x', 'z'), 0, 0, tiled=True)]
    pallas_call x1, Pallas kernels: 68.9 us -> 118 us  [shampoo(): pl.pallas_call(functools.partial(step_kernel, sizes), out_shape=(jax.Shap...]
    all_to_all x3 -> x0, starting transfers between devices: 15.5 us -> none  [the longest x1 6.29 us: per_device(): extra = lax.all_to_all(extra, ('x', 'z'), 0, 0, tiled=True)]
    dot_general x6 -> x0, matrix products: 14.9 us -> none  [the longest x4 11.1 us: product(): return jnp.einsum('...ij,...jk->...ik', left, right, precision=HIGH)]
    unnamed x22 -> x9, local copies, waits for them, and re-layouts: 12.2 us -> 9.31 us
  transfers between devices with their start and end apart: 3 -> 0, of which waited for: 3 -> 0; matrix products, arithmetic and copies ran while one was open for 7% -> 0% of each run, Pallas kernels for 0% -> 0%
where the time goes in v3:
time: 133 us
  Pallas kernels  118 us (89%)
  local copies, waits for them, and re-layouts  9.98 us (8%)
  other arithmetic  4.04 us (3%)
    pallas_call x1, Pallas kernels, shampoo(): pl.pallas_call(functools.partial(step_kernel, sizes), out_shape=(jax.Shap...  118 us
    unnamed x9, local copies, waits for them, and re-layouts  9.31 us

profile of v3, /device:TPU:8, one launch (start us, length us, event | category | flops | bytes accessed | tf_op | source)
XLA Modules:
  0.0 133.1 jit_solution(4641499817231378670)
XLA Ops:
  0.6 0.9 convert_reduce_fusion
  1.6 0.7 fusion.1
  2.2 1.2 multiply_add_fusion.targets
  3.4 0.2 compare_reduce_fusion
  3.6 0.6 select_reduce_fusion.source
  4.2 0.5 convert_element_type.7.used
  4.7 1.0 copy.15
  5.7 0.7 copy.16
  6.4 118.4 %shard_map.93 = (bf16[32,16,512]{2,1,0:T(8,128)(2,1)}, f32[2,512,512]{2,1,0:T(8,128)}, f32[2,512,512]{2,1,0:T(8,128)}, f32[512,512]{1,0:T(8,128)}) custom-call(bf16[8,64,128]{2,1,0:T(8,128)(2,1)} %bitcast.29, bf16[128,2048]{1,0:T(8,128)(2,1)} %cot.1, f32[2,512,512]{2,1,0:T(8,128)} %bitcast.23, f32[2,512,512]{2,1,0:T(8,128)} %bitcast.24, ...), custom_call_target="tpu_custom_call" | custom-call | tf_op jit(solution)/shard_map/pallas_call | solution.py:513
  124.8 2.1 %copy.17 = bf16[1,16,32,512]{3,2,1,0:T(8,128)(2,1)} copy(bf16[1,16,32,512]{3,1,2,0:T(8,128)(2,1)} %bitcast.30) | data formatting | bytes 1048576
  126.9 0.0 copy-start
  126.9 3.2 %copy.21 = f32[1,1,2,512,512]{4,3,2,1,0:T(8,128)} copy(f32[1,1,2,512,512]{4,3,2,1,0:T(8,128)} %bitcast.26) | data formatting | bytes 4194304
  130.2 0.0 copy-done
  130.2 0.0 copy-start.1
  130.2 1.3 copy.22
  131.5 0.6 copy-done.1
  132.1 1.0 copy.23
  (1 shorter events, 0.0 us)
Async XLA Ops:
  126.9 3.2 %copy-start = (f32[2,512,512]{2,1,0:T(8,128)S(1)}, f32[2,512,512]{2,1,0:T(8,128)}, u32[]{:S(2)}) copy-start(f32[2,512,512]{2,1,0:T(8,128)} %get-tuple-element.10) | copy-start | bytes 6291460
  130.2 2.0 %copy-start.1 = (f32[512,512]{1,0:T(8,128)S(1)}, f32[512,512]{1,0:T(8,128)}, u32[]{:S(2)}) copy-start(f32[512,512]{1,0:T(8,128)} %get-tuple-element.11) | copy-start | bytes 3145732

commit v4 on v3

--- a/solution.py
+++ b/solution.py
@@ -37,9 +37,9 @@
 
 
 def step_kernel(
-    sizes, act, cot, stats_left, stats_right, variance, source, targets, used,
+    sizes, act, cot, stats_left, stats_right, variance, owners,
     direction, left_new, right_new, var_new,
-    cbuf, abuf, grad, sbuf, vbuf, vt, matrix, m2, m_h, m_l, m2_h, m2_l, w_h, w_l, root_h, root_l,
+    act_in, act_t, source, targets, used, cbuf, abuf, grad, sbuf, vbuf, vt, matrix, m2, m_h, m_l, m2_h, m2_l, w_h, w_l, root_h, root_l,
     gsend, gsend_row, gq, gq_row, scale_rows, adam_rows, send_q, send_row, rq, rq_row,
     owned_h, owned_l, pre, finished, ret,
     own_sem, stat_sem, out_sem, var_sem, c1_s, c1_r, a1_s, a1_r, zr_s, zr_r, a2_s, a2_r,
@@ -60,6 +60,17 @@
             device_id=where, device_id_type=MESH,
         )
 
+    barrier = pltpu.get_barrier_semaphore()
+
+    def plane(d):
+        return lax.rem(x + d // nz, nx), lax.rem(z + lax.rem(d, nz), nz)
+
+    partners = [{"x": lax.rem(x + d, nx)} for d in range(1, nx)]
+    partners += [{"z": lax.rem(z + d, nz)} for d in range(1, nz)]
+    partners += [{"y": lax.rem(y + d, ny)} for d in range(1, ny)]
+    partners += [{"c": 1 - c}]
+    for partner in partners:
+        pl.semaphore_signal(barrier, inc=1, device_id=partner, device_id_type=MESH)
     loads = [
         pltpu.make_async_copy(ref.at[slot], sbuf.at[2 * side + slot], stat_sem.at[2 * side + slot])
         for side, ref in enumerate((stats_left, stats_right))
@@ -68,34 +79,26 @@
     own_c = pltpu.make_async_copy(
         cot.at[:, pl.ds(pl.multiple_of(x * block, block), block)], cbuf.at[z, x], own_sem.at[0]
     )
-    own_a = pltpu.make_async_copy(act.at[z], abuf.at[z, x, mine], own_sem.at[1])
+    act_load = pltpu.make_async_copy(act, act_in, own_sem.at[1])
     loads += [
         pltpu.make_async_copy(
             variance.at[:, k * lane : (k + 1) * lane], vbuf.at[k], var_sem.at[0, k]
         )
         for k in range(block // lane)
     ]
+    act_load.start()
     own_c.start()
-    own_a.start()
     for load in loads:
         load.start()
 
-    barrier = pltpu.get_barrier_semaphore()
-
-    def plane(d):
-        return lax.rem(x + d // nz, nx), lax.rem(z + lax.rem(d, nz), nz)
-
-    def greet(d, carry):
-        x2, z2 = plane(d)
-        pl.semaphore_signal(barrier, inc=1, device_id={"x": x2, "z": z2}, device_id_type=MESH)
-        return carry
-
-    lax.fori_loop(1, devices, greet, 0)
-    partners = [{"y": lax.rem(y + d, ny)} for d in range(1, ny)]
-    partners += [{"c": 1 - c}]
-    for partner in partners:
-        pl.semaphore_signal(barrier, inc=1, device_id=partner, device_id_type=MESH)
-    pl.semaphore_wait(barrier, len(partners) + devices - 1)
+    act_load.wait()
+    turned = act_in[...].T
+    for x2 in range(nx):
+        for z2 in range(nz):
+            first = (x2 * nz + z2) * strip
+            act_t[z2, x2 * strip : (x2 + 1) * strip, :] = turned[first : first + strip]
+    abuf[z, x, mine] = act_t[z]
+    pl.semaphore_wait(barrier, len(partners))
 
     sends = []
 
@@ -112,7 +115,7 @@
 
     def a1(d):
         z2 = lax.rem(z + d, nz)
-        return remote(act.at[z2], abuf.at[z, x, mine], a1_s.at[d - 1], a1_r.at[d - 1], z=z2)
+        return remote(act_t.at[z2], abuf.at[z, x, mine], a1_s.at[d - 1], a1_r.at[d - 1], z=z2)
 
     def ring(way, hop, k):
         x2 = lax.rem(x - k + nx, nx)
@@ -137,18 +140,22 @@
         part = abuf.at[:, lax.rem(x - k + nx, nx), 2 * lax.rem(y - d + ny, ny) + c]
         return remote(part, part, sib_s.at[k, d], sib_r.at[k, d], c=1 - c)
 
-    for d in range(1, nx):
-        launch(c1(d))
+    near = [1, nx - 1]
+    for d in near:
+        c1(d).start()
     own_c.wait()
     for way in range(2):
         launch(ring(way, 0, 0))
     for d in range(1, nz):
         launch(a1(d))
-    for k in range(1, nx):
+    for d in near:
+        c1(d).wait_send()
+    for d in range(2, nx - 1):
+        launch(c1(d))
+    for k in near + list(range(2, nx - 1)):
         c1(k).wait_recv()
         for way in range(2):
             launch(ring(way, 0, k))
-    own_a.wait()
     for d in range(1, nz):
         a1(d).wait_recv()
     for d in range(1, nx):
@@ -159,22 +166,47 @@
     for load in loads:
         load.wait()
 
+    def find_blocks(owner, carry):
+        low, high = jnp.int32(count), jnp.int32(0)
+        for b in range(count):
+            hit = owners[b] == owner
+            low = jnp.where(hit, jnp.minimum(low, b), low)
+            high = jnp.where(hit, b, high)
+        source[2 * owner] = jnp.where(low == count, 0, low)
+        source[2 * owner + 1] = high
+        return carry
+
+    def find_target(b, carry):
+        earlier = jnp.int32(0)
+        for c2 in range(count):
+            hit = jnp.logical_and(owners[c2] == owners[b], c2 < b)
+            earlier = jnp.where(hit, earlier + 1, earlier)
+        targets[b] = 2 * owners[b] + earlier
+        return carry
+
+    held = jnp.int32(0)
+    for b in range(count):
+        held = jnp.where(owners[b] == me, held + 1, held)
+    for slot in range(2):
+        used[slot] = jnp.where(held > slot, 1.0, 0.0)
+
     items = nx * (ny - 1)
     per_step = -(-items // 6)
 
     def one_matrix(q, carry):
         for t in range(3):
             n = 3 * q + t
-            hop, k = n // nx + 1, lax.rem(n, nx)
+            hop, place = n // nx + 1, lax.rem(n, nx)
+            k = jnp.where(place == 2, nx - 1, jnp.where(place == 3, 2, place))
             ring(0, hop - 1, k).wait_recv()
             ring(1, hop - 1, k).wait_recv()
             inner = hop < half - 1
 
-            @pl.when(jnp.logical_or(inner, k < nx // 2))
+            @pl.when(jnp.logical_or(inner, place < nx // 2))
             def _():
                 ring(0, hop, k).start()
 
-            @pl.when(jnp.logical_or(inner, k >= nx // 2))
+            @pl.when(jnp.logical_or(inner, place >= nx // 2))
             def _():
                 ring(1, hop, k).start()
 
@@ -195,6 +227,11 @@
                     k2, d2 = item // (ny - 1), lax.rem(item, ny - 1) + 1
                     over_y(k2, d2).wait_recv()
                     sibling(k2, d2).start()
+
+            each = -(-devices // 12)
+            lax.fori_loop(n * each, jnp.minimum(n * each + each, devices), find_blocks, 0)
+            each = -(-count // 12)
+            lax.fori_loop(n * each, jnp.minimum(n * each + each, count), find_target, 0)
 
             if t == 0:
                 stat = sbuf[q]
@@ -279,7 +316,7 @@
     diagonal = lax.broadcasted_iota(jnp.int32, (width, width), 0) == lax.broadcasted_iota(
         jnp.int32, (width, width), 1
     )
-    for d in list(range(1, nx)) + [0]:
+    for d in [2, 1, nx - 1, 0]:
         j = lax.rem(x + d, nx)
         rows = pl.ds(pl.multiple_of(j * strip, strip), strip)
         value = grad[:, rows, :].reshape(width, block) + shard(far, rows)
@@ -317,7 +354,7 @@
             scale_rows[pl.ds(b, 1), :] = jnp.where(inside, row, 0.0)
 
     strips_of(x)
-    for d in range(1, nx):
+    for d in (1, nx - 1, 2):
         for copy in exchange(d):
             copy.wait_recv()
         strips_of(lax.rem(x - d + nx, nx))
@@ -495,11 +532,12 @@
                 sibling(k, d).wait_send()
 
 
-def shampoo(act, cot, stats_left, stats_right, variance, source, targets, used):
-    nz, rows_z, tokens = act.shape
-    nx, ny = lax.axis_size("x"), lax.axis_size("y")
+def shampoo(act, cot, stats_left, stats_right, variance, owners):
+    tokens = act.shape[0]
+    nx, nz, ny = lax.axis_size("x"), lax.axis_size("z"), lax.axis_size("y")
     block = stats_left.shape[-1]
-    strip = rows_z // nx
+    strip = block // (nx * nz)
+    rows_z = nx * strip
     rows_i = 2 * ny
     sizes = (nx, nz, ny, block, strip, tokens, rows_i)
     half = nz // 2
@@ -518,9 +556,14 @@
             jax.ShapeDtypeStruct(stats_right.shape, f32),
             jax.ShapeDtypeStruct(variance.shape, f32),
         ),
-        in_specs=[anywhere] * 5 + [scalars] * 3,
+        in_specs=[anywhere] * 5 + [scalars],
         out_specs=(pl.BlockSpec(memory_space=pltpu.VMEM),) + (anywhere,) * 3,
         scratch_shapes=[
+            vmem((tokens, block), bf16),
+            vmem((nz, rows_z, tokens), bf16),
+            pltpu.SMEM((2 * devices,), jnp.int32),
+            pltpu.SMEM((count,), jnp.int32),
+            pltpu.SMEM((2,), f32),
             vmem((nz, nx, tokens, block), bf16),
             vmem((nz, nx, rows_i, rows_z, tokens), bf16),
             vmem((rows_i, rows_z, block), f32),
@@ -562,39 +605,54 @@
         compiler_params=pltpu.CompilerParams(
             collective_id=0, has_side_effects=True, vmem_limit_bytes=60 * 1024 * 1024
         ),
-    )(act, cot, stats_left, stats_right, variance, source, targets, used)
-
-
-def slot_targets(owner_ids, capacity):
-    count = owner_ids.shape[-1]
-    matching = owner_ids[:, None] == owner_ids[None, :]
-    earlier = jnp.arange(count)[None, :] < jnp.arange(count)[:, None]
-    slots = jnp.sum(jnp.logical_and(matching, earlier), axis=-1)
-    return owner_ids * capacity + slots
+    )(act, cot, stats_left, stats_right, variance, owners)
+
+
+def settle_kernel(left, right, variance, left_out, right_out, variance_out, held, in_sem, out_sem):
+    pairs = [(left.at[s], left_out.at[s]) for s in range(left.shape[0])]
+    pairs += [(right.at[s], right_out.at[s]) for s in range(right.shape[0])]
+    pairs += [(variance, variance_out)]
+    reads = [
+        pltpu.make_async_copy(src, held.at[k], in_sem.at[k]) for k, (src, _) in enumerate(pairs)
+    ]
+    writes = [
+        pltpu.make_async_copy(held.at[k], dst, out_sem.at[k]) for k, (_, dst) in enumerate(pairs)
+    ]
+    for copy in reads:
+        copy.start()
+    for read, write in zip(reads, writes):
+        read.wait()
+        write.start()
+    for copy in writes:
+        copy.wait()
+
+
+def settle(left, right, variance):
+    pieces = 2 * left.shape[0] + 1
+    anywhere = pl.BlockSpec(memory_space=pl.ANY)
+    return pl.pallas_call(
+        settle_kernel,
+        out_shape=tuple(jax.ShapeDtypeStruct(a.shape, a.dtype) for a in (left, right, variance)),
+        in_specs=[anywhere] * 3,
+        out_specs=(anywhere,) * 3,
+        scratch_shapes=[
+            pltpu.VMEM((pieces,) + variance.shape, variance.dtype),
+            pltpu.SemaphoreType.DMA((pieces,)),
+            pltpu.SemaphoreType.DMA((pieces,)),
+        ],
+        compiler_params=pltpu.CompilerParams(vmem_limit_bytes=60 * 1024 * 1024),
+    )(left, right, variance)
 
 
 def per_device(activations, cotangents, owners, stats_left, stats_right, variance):
-    tokens, block = activations.shape
+    block = activations.shape[1]
     count = owners.shape[0]
-    capacity = stats_left.shape[2]
-    devices = lax.axis_size("x") * lax.axis_size("z")
-    strip = block // devices
-
-    targets = slot_targets(owners[:, 0], capacity)
-    slot_ids = jnp.arange(devices * capacity, dtype=jnp.int32)
-    select = targets[:, None] == slot_ids[None, :]
-    blocks = jnp.arange(count, dtype=jnp.int32)
-    source = jnp.sum(jnp.where(select, blocks[:, None], 0), axis=0)
-    me = lax.axis_index("x") * lax.axis_size("z") + lax.axis_index("z")
-    mine = me * capacity + jnp.arange(capacity, dtype=jnp.int32)
-    used = jnp.any(targets[:, None] == mine[None, :], axis=0).astype(jnp.float32)
-
-    act = activations.T.reshape(-1, lax.axis_size("z"), strip, tokens).transpose(1, 0, 2, 3)
-    act = act.reshape(lax.axis_size("z"), -1, tokens)
+    strip = variance.shape[1]
     direction, left_new, right_new, var_new = shampoo(
-        act, cotangents, stats_left[0, 0], stats_right[0, 0],
-        variance.reshape(strip * count, block), source, targets, used,
+        activations, cotangents, stats_left[0, 0], stats_right[0, 0],
+        variance.reshape(strip * count, block), owners[:, 0],
     )
+    left_new, right_new, var_new = settle(left_new, right_new, var_new)
     direction = direction.transpose(1, 0, 2)[None]
     return (direction, left_new[None, None], right_new[None, None], var_new.reshape(variance.shape))
 

time: 133 us -> 125 us (0.940)
  local copies, waits for them, and re-layouts: 9.98 us -> 2.13 us
  other arithmetic: 4.04 us -> 0 us
  Pallas kernels: 118 us -> 122 us
    unnamed x9 -> x1, local copies, waits for them, and re-layouts: 9.31 us -> 2.13 us
    pallas_call x0 -> x1, Pallas kernels: none -> 4.37 us  [settle(): pl.pallas_call(settle_kernel, out_shape=tuple((jax.ShapeDtypeStruct(a.sha...]
    reduce_sum x2 -> x0, other arithmetic: 1.51 us -> none  [the longest x1 0.91 us: slot_targets(): slots = jnp.sum(jnp.logical_and(matching, earlier), axis=-1)]
where the time goes in v4:
time: 125 us
  Pallas kernels  122 us (98%)
  local copies, waits for them, and re-layouts  2.13 us (2%)
    pallas_call x1, Pallas kernels, shampoo(): pl.pallas_call(functools.partial(step_kernel, sizes), out_shape=(jax.Shap...  118 us
    pallas_call x1, Pallas kernels, settle(): pl.pallas_call(settle_kernel, out_shape=tuple((jax.ShapeDtypeStruct(a.sha...  4.37 us

profile of v4, /device:TPU:8, one launch (start us, length us, event | category | flops | bytes accessed | tf_op | source)
XLA Modules:
  0.0 124.7 jit_solution(1448040537094154601)
XLA Ops:
  0.6 117.6 %shard_map.93 = (bf16[32,16,512]{2,1,0:T(8,128)(2,1)}, f32[2,512,512]{2,1,0:T(8,128)}, f32[2,512,512]{2,1,0:T(8,128)}, f32[512,512]{1,0:T(8,128)}) custom-call(bf16[128,512]{1,0:T(8,128)(2,1)} %act.1, bf16[128,2048]{1,0:T(8,128)(2,1)} %cot.1, f32[2,512,512]{2,1,0:T(8,128)} %bitcast.10, f32[2,512,512]{2,1,0:T(8,128)} %bitcast.11, f32[512,512]{1,0:T(8,128)} %bitcast.12, ...), custom_call_target="tpu_custom_call" | custom-call | tf_op jit(solution)/shard_map/pallas_call | solution.py:551
  118.2 2.1 %copy.10 = bf16[1,16,32,512]{3,2,1,0:T(8,128)(2,1)} copy(bf16[1,16,32,512]{3,1,2,0:T(8,128)(2,1)} %bitcast.13) | data formatting | bytes 1048576
  120.3 4.4 %shard_map.94 = (f32[2,512,512]{2,1,0:T(8,128)}, f32[2,512,512]{2,1,0:T(8,128)}, f32[512,512]{1,0:T(8,128)}) custom-call(f32[2,512,512]{2,1,0:T(8,128)} %get-tuple-element.12.left, f32[2,512,512]{2,1,0:T(8,128)} %get-tuple-element.13.right, f32[512,512]{1,0:T(8,128)} %get-tuple-element.14.variance), custom_call_target="tpu_custom_call" | custom-call | tf_op jit(solution)/shard_map/pallas_call | solution.py:633

commit v5 on v4

--- a/solution.py
+++ b/solution.py
@@ -61,9 +61,6 @@
         )
 
     barrier = pltpu.get_barrier_semaphore()
-
-    def plane(d):
-        return lax.rem(x + d // nz, nx), lax.rem(z + lax.rem(d, nz), nz)
 
     partners = [{"x": lax.rem(x + d, nx)} for d in range(1, nx)]
     partners += [{"z": lax.rem(z + d, nz)} for d in range(1, nz)]
@@ -359,33 +356,66 @@
             copy.wait_recv()
         strips_of(lax.rem(x - d + nx, nx))
 
-    def go(slot, d):
-        x2, z2 = plane(d)
-        other = x2 * nz + z2
-        return (
-            remote(send_q.at[slot, other], rq.at[slot, me],
-                   go_s.at[slot, d - 1], go_r.at[slot, d - 1], x=x2, z=z2),
-            remote(send_row.at[slot, other], rq_row.at[slot, me],
-                   gor_s.at[slot, d - 1], gor_r.at[slot, d - 1], x=x2, z=z2),
+    def wrapped(value, size):
+        return jnp.where(value >= size, value - size, value)
+
+    turns = [half] + [dz for step in range(1, half) for dz in (step, nz - step)]
+
+    def others(body, sign):
+        ends = {dz: wrapped(z + (dz if sign > 0 else nz - dz), nz) for dz in turns}
+
+        def one(dx, carry):
+            x2 = wrapped(x + (dx if sign > 0 else nx - dx), nx)
+            for dz in turns:
+                body(dx * nz + dz, x2, ends[dz])
+
+            @pl.when(dx > 0)
+            def _():
+                body(dx * nz, x2, z)
+
+            return carry
+
+        lax.fori_loop(0, nx, one, 0)
+
+    def go(slot, d, x2, z2):
+        return remote(
+            send_q.at[slot, x2 * nz + z2], rq.at[slot, me],
+            go_s.at[slot, d - 1], go_r.at[slot, d - 1], x=x2, z=z2,
+        )
+
+    def go_row(d, x2, z2):
+        return remote(
+            send_row.at[x2 * nz + z2], rq_row.at[me], gor_s.at[d - 1], gor_r.at[d - 1], x=x2, z=z2
         )
 
     def picked(slot, other):
         b = source[2 * other + slot]
-        rows = jnp.concatenate([scale_rows[pl.ds(b, 1), :], adam_rows[pl.ds(b, 1), :]], axis=0)
-        return gq[lax.rem(b, nx), b // nx], rows
+        return gq[lax.rem(b, nx), b // nx]
+
+    def picked_rows(other):
+        return jnp.concatenate(
+            [
+                rows[pl.ds(source[2 * other + slot], 1), :]
+                for slot in range(2)
+                for rows in (scale_rows, adam_rows)
+            ],
+            axis=0,
+        )
 
     for slot in range(2):
 
-        def send(d, carry):
-            x2, z2 = plane(d)
+        def send(d, x2, z2):
             other = x2 * nz + z2
-            send_q[slot, other], send_row[slot, other] = picked(slot, other)
-            for copy in go(slot, d):
-                copy.start()
-            return carry
-
-        lax.fori_loop(1, devices, send, 0)
-        rq[slot, me], rq_row[slot, me] = picked(slot, me)
+            send_q[slot, other] = picked(slot, other)
+            go(slot, d, x2, z2).start()
+            if slot == 0:
+                send_row[other] = picked_rows(other)
+                go_row(d, x2, z2).start()
+
+        others(send, 1)
+        rq[slot, me] = picked(slot, me)
+        if slot == 0:
+            rq_row[me] = picked_rows(me)
 
     def reorder(r, carry):
         rows = pl.ds(pl.multiple_of(r * count, count), count)
@@ -403,13 +433,8 @@
     for copy in outs:
         copy.start()
 
-    def arrival(d):
-        return lax.rem(x - d // nz + nx, nx) * nz + lax.rem(z - lax.rem(d, nz) + nz, nz)
-
-    def back(slot, d):
-        x2, z2 = plane(d)
-        other = x2 * nz + z2
-        rows = pl.ds(pl.multiple_of(other * strip, strip), strip)
+    def back(slot, d, x2, z2):
+        rows = pl.ds(pl.multiple_of((x2 * nz + z2) * strip, strip), strip)
         return remote(
             finished.at[slot, rows, :], ret.at[2 * me + slot],
             back_s.at[slot, d - 1], back_r.at[slot, d - 1], x=x2, z=z2,
@@ -421,21 +446,22 @@
     for slot in range(2):
         keep = used[slot]
 
-        def decode(p, total):
-            extra = rq_row[slot, p]
-            column = jnp.sum(jnp.where(fits, extra[0:1], 0.0), axis=1, keepdims=True) * keep
+        def decode(p):
+            row = rq_row[p, 2 * slot : 2 * slot + 1]
+            column = jnp.sum(jnp.where(fits, row, 0.0), axis=1, keepdims=True) * keep
             value = rq[slot, p].astype(jnp.float32) * column
             rows = pl.ds(pl.multiple_of(p * strip, strip), strip)
             owned_h[slot, rows, :], owned_l[slot, rows, :] = halves(value)
-            return total + extra[1:2]
-
-        def receive(d, total):
-            for copy in go(slot, d):
-                copy.wait_recv()
-            return decode(arrival(d), total)
-
-        total = decode(me, jnp.zeros((1, width), jnp.float32))
-        total = lax.fori_loop(1, devices, receive, total)
+
+        def receive(d, x2, z2):
+            if slot == 0:
+                go_row(d, x2, z2).wait_recv()
+            go(slot, d, x2, z2).wait_recv()
+            decode(x2 * nz + z2)
+
+        decode(me)
+        others(receive, -1)
+        total = jnp.sum(rq_row[:, 2 * slot + 1 : 2 * slot + 2, :], axis=0)
 
         def finish(rows, value):
             m_h[rows, :], m_l[rows, :] = halves(value)
@@ -454,11 +480,7 @@
         ratio = jnp.sqrt(mean_adam / (squares * (1.0 / (block * block)) + 1e-6))
         finished[slot] = (value * ratio).astype(jnp.bfloat16)
 
-        def send_back(d, carry):
-            back(slot, d).start()
-            return carry
-
-        lax.fori_loop(1, devices, send_back, 0)
+        others(lambda d, x2, z2: back(slot, d, x2, z2).start(), 1)
         rows = pl.ds(pl.multiple_of(me * strip, strip), strip)
         ret[2 * me + slot] = finished[slot, rows, :]
 
@@ -492,12 +514,7 @@
             copy.start()
 
     for slot in range(2):
-
-        def collect(d, carry):
-            back(slot, d).wait_recv()
-            return carry
-
-        lax.fori_loop(1, devices, collect, 0)
+        others(lambda d, x2, z2: back(slot, d, x2, z2).wait_recv(), -1)
 
     def choose(b, carry):
         direction[b] = ret[targets[b]]
@@ -508,14 +525,9 @@
     for copy in outs:
         copy.wait()
     for slot in range(2):
-
-        def drain(d, carry):
-            for copy in go(slot, d):
-                copy.wait_send()
-            back(slot, d).wait_send()
-            return carry
-
-        lax.fori_loop(1, devices, drain, 0)
+        others(lambda d, x2, z2: go(slot, d, x2, z2).wait_send(), 1)
+        others(lambda d, x2, z2: back(slot, d, x2, z2).wait_send(), 1)
+    others(lambda d, x2, z2: go_row(d, x2, z2).wait_send(), 1)
     for copy in sends:
         copy.wait_send()
     for hop in range(1, half):
@@ -584,9 +596,9 @@
             vmem((count, width), f32),
             vmem((count, width), f32),
             vmem((2, devices, strip, block), i16),
-            vmem((2, devices, 2, width), f32),
+            vmem((devices, 4, width), f32),
             vmem((2, devices, strip, block), i16),
-            vmem((2, devices, 2, width), f32),
+            vmem((devices, 4, width), f32),
             vmem((2, block, block), bf16),
             vmem((2, block, block), bf16),
             vmem(square, f32),
@@ -601,47 +613,81 @@
             sem((nx, ny)), sem((nx, ny)),
         ]
         + [sem((nx - 1,))] * 4
-        + [sem((2, devices - 1))] * 6,
+        + [sem((2, devices - 1))] * 2
+        + [sem((devices - 1,))] * 2
+        + [sem((2, devices - 1))] * 2,
         compiler_params=pltpu.CompilerParams(
             collective_id=0, has_side_effects=True, vmem_limit_bytes=60 * 1024 * 1024
         ),
     )(act, cot, stats_left, stats_right, variance, owners)
 
 
-def settle_kernel(left, right, variance, left_out, right_out, variance_out, held, in_sem, out_sem):
-    pairs = [(left.at[s], left_out.at[s]) for s in range(left.shape[0])]
-    pairs += [(right.at[s], right_out.at[s]) for s in range(right.shape[0])]
-    pairs += [(variance, variance_out)]
+def settle_kernel(
+    left, right, variance, direction, left_out, right_out, variance_out, direction_out,
+    held, taken, spread, turned, in_sem, out_sem, way_sem,
+):
+    block = variance.shape[1]
+    count, strip = direction.shape[:2]
+    lane = spread.shape[2]
+    per, part = held.shape[0] // 5, held.shape[1]
+    pairs = []
+    for step in range(per):
+        rows = pl.ds(step * part, part)
+        for src, dst in ((left, left_out), (right, right_out)):
+            pairs += [(src.at[s, rows, :], dst.at[s, rows, :]) for s in range(2)]
+        pairs += [(variance.at[rows, :], variance_out.at[rows, :])]
+    first = pltpu.make_async_copy(direction, taken, way_sem.at[0])
+    last = pltpu.make_async_copy(turned, direction_out, way_sem.at[1])
     reads = [
         pltpu.make_async_copy(src, held.at[k], in_sem.at[k]) for k, (src, _) in enumerate(pairs)
     ]
     writes = [
         pltpu.make_async_copy(held.at[k], dst, out_sem.at[k]) for k, (_, dst) in enumerate(pairs)
     ]
+    first.start()
     for copy in reads:
         copy.start()
-    for read, write in zip(reads, writes):
-        read.wait()
-        write.start()
+    for k in range(len(pairs) // 2):
+        reads[k].wait()
+        writes[k].start()
+    first.wait()
+    value = taken[...].reshape(count * strip, block).astype(jnp.float32)
+    for k in range(block // lane):
+        spread[k] = value[:, k * lane : (k + 1) * lane]
+    for r in range(strip):
+        turned[r] = jnp.concatenate(
+            [spread[k, pl.ds(r, count, stride=strip), :] for k in range(block // lane)], axis=1
+        ).astype(turned.dtype)
+    last.start()
+    for k in range(len(pairs) // 2, len(pairs)):
+        reads[k].wait()
+        writes[k].start()
     for copy in writes:
         copy.wait()
-
-
-def settle(left, right, variance):
-    pieces = 2 * left.shape[0] + 1
+    last.wait()
+
+
+def settle(left, right, variance, direction):
+    count, strip, block = direction.shape
+    lane, part = min(block, 128), block // 4
+    pieces = 5 * (block // part)
     anywhere = pl.BlockSpec(memory_space=pl.ANY)
+    vmem, sem = pltpu.VMEM, pltpu.SemaphoreType.DMA
     return pl.pallas_call(
         settle_kernel,
-        out_shape=tuple(jax.ShapeDtypeStruct(a.shape, a.dtype) for a in (left, right, variance)),
-        in_specs=[anywhere] * 3,
-        out_specs=(anywhere,) * 3,
+        out_shape=tuple(jax.ShapeDtypeStruct(a.shape, a.dtype) for a in (left, right, variance))
+        + (jax.ShapeDtypeStruct((strip, count, block), direction.dtype),),
+        in_specs=[anywhere] * 4,
+        out_specs=(anywhere,) * 4,
         scratch_shapes=[
-            pltpu.VMEM((pieces,) + variance.shape, variance.dtype),
-            pltpu.SemaphoreType.DMA((pieces,)),
-            pltpu.SemaphoreType.DMA((pieces,)),
+            vmem((pieces, part, block), variance.dtype),
+            vmem(direction.shape, direction.dtype),
+            vmem((block // lane, count * strip, lane), jnp.float32),
+            vmem((strip, count, block), direction.dtype),
+            sem((pieces,)), sem((pieces,)), sem((2,)),
         ],
         compiler_params=pltpu.CompilerParams(vmem_limit_bytes=60 * 1024 * 1024),
-    )(left, right, variance)
+    )(left, right, variance, direction)
 
 
 def per_device(activations, cotangents, owners, stats_left, stats_right, variance):
@@ -652,9 +698,8 @@
         activations, cotangents, stats_left[0, 0], stats_right[0, 0],
         variance.reshape(strip * count, block), owners[:, 0],
     )
-    left_new, right_new, var_new = settle(left_new, right_new, var_new)
-    direction = direction.transpose(1, 0, 2)[None]
-    return (direction, left_new[None, None], right_new[None, None], var_new.reshape(variance.shape))
+    left_new, right_new, var_new, direction = settle(left_new, right_new, var_new, direction)
+    return (direction[None], left_new[None, None], right_new[None, None], var_new.reshape(variance.shape))
 
 
 def solution(mesh):

time: 125 us -> 123 us (0.984)
  local copies, waits for them, and re-layouts: 2.13 us -> 0 us
    unnamed x1 -> x0, local copies, waits for them, and re-layouts: 2.13 us -> none
    pallas_call x1, Pallas kernels: 118 us -> 116 us  [shampoo(): pl.pallas_call(functools.partial(step_kernel, sizes), out_shape=(jax.Shap...]
    pallas_call x1, Pallas kernels: 4.37 us -> 5.88 us  [settle(): pl.pallas_call(settle_kernel, out_shape=tuple((jax.ShapeDtypeStruct(a.sha...]
where the time goes in v5:
time: 123 us; the launch traced here: 122 us
  Pallas kernels  122 us (99%)
    pallas_call x1, Pallas kernels, shampoo(): pl.pallas_call(functools.partial(step_kernel, sizes), out_shape=(jax.Shap...  116 us
    pallas_call x1, Pallas kernels, settle(): pl.pallas_call(settle_kernel, out_shape=tuple((jax.ShapeDtypeStruct(a.sha...  5.88 us

profile of v5, /device:TPU:8, one launch (start us, length us, event | category | flops | bytes accessed | tf_op | source)
XLA Modules:
  0.0 122.5 jit_solution(10307945918816431741)
XLA Ops:
  0.6 116.0 %shard_map.93 = (bf16[32,16,512]{2,1,0:T(8,128)(2,1)}, f32[2,512,512]{2,1,0:T(8,128)}, f32[2,512,512]{2,1,0:T(8,128)}, f32[512,512]{1,0:T(8,128)}) custom-call(bf16[128,512]{1,0:T(8,128)(2,1)} %act.1, bf16[128,2048]{1,0:T(8,128)(2,1)} %cot.1, f32[2,512,512]{2,1,0:T(8,128)} %bitcast.8, f32[2,512,512]{2,1,0:T(8,128)} %bitcast.9, f32[512,512]{1,0:T(8,128)} %bitcast.10, ...), custom_call_target="tpu_custom_call" | custom-call | tf_op jit(solution)/shard_map/pallas_call | solution.py:563
  116.6 5.9 %shard_map.94 = (f32[2,512,512]{2,1,0:T(8,128)}, f32[2,512,512]{2,1,0:T(8,128)}, f32[512,512]{1,0:T(8,128)}, bf16[16,32,512]{2,1,0:T(8,128)(2,1)}) custom-call(f32[2,512,512]{2,1,0:T(8,128)} %get-tuple-element.12.left, f32[2,512,512]{2,1,0:T(8,128)} %get-tuple-element.13.right, f32[512,512]{1,0:T(8,128)} %get-tuple-element.14.variance, ...), custom_call_target="tpu_custom_call" | custom-call | tf_op jit(solution)/shard_map/pallas_call | solution.py:676

commit v6 on v5

--- a/solution.py
+++ b/solution.py
@@ -88,6 +88,55 @@
     for load in loads:
         load.start()
 
+    pl.semaphore_wait(barrier, len(partners))
+
+    sends = []
+
+    def launch(copy):
+        copy.start()
+        sends.append(copy)
+
+    def c1(d):
+        j = lax.rem(x + d, nx)
+        return remote(
+            cot.at[:, pl.ds(pl.multiple_of(j * block, block), block)],
+            cbuf.at[z, x], c1_s.at[d - 1], c1_r.at[d - 1], x=j,
+        )
+
+    def a1(d):
+        z2 = lax.rem(z + d, nz)
+        return remote(act_t.at[z2], abuf.at[z, x, mine], a1_s.at[d - 1], a1_r.at[d - 1], z=z2)
+
+    own = cot.at[:, pl.ds(pl.multiple_of(x * block, block), block)]
+
+    def ring(way, hop, k, held=None):
+        x2 = lax.rem(x - k + nx, nx)
+        step = 1 if way == 0 else nz - 1
+        origin = lax.rem(z - hop + nz, nz) if way == 0 else lax.rem(z + hop, nz)
+        part = cbuf.at[origin, x2]
+        return remote(
+            part if held is None else held, part, zr_s.at[way, hop, k], zr_r.at[way, hop, k], z=lax.rem(z + step, nz)
+        )
+
+    def a2(d):
+        part = abuf.at[:, x, mine]
+        return remote(part, part, a2_s.at[d - 1], a2_r.at[d - 1], x=lax.rem(x + d, nx))
+
+    def over_y(k, d):
+        part = abuf.at[:, lax.rem(x - k + nx, nx), mine]
+        return remote(
+            part, part, y_s.at[k, d - 1], y_r.at[k, d - 1], y=lax.rem(y + d, ny)
+        )
+
+    def sibling(k, d):
+        part = abuf.at[:, lax.rem(x - k + nx, nx), 2 * lax.rem(y - d + ny, ny) + c]
+        return remote(part, part, sib_s.at[k, d], sib_r.at[k, d], c=1 - c)
+
+    near = [1, nx - 1]
+    for d in near:
+        c1(d).start()
+    for way in range(2):
+        launch(ring(way, 0, 0, own))
     act_load.wait()
     turned = act_in[...].T
     for x2 in range(nx):
@@ -95,54 +144,6 @@
             first = (x2 * nz + z2) * strip
             act_t[z2, x2 * strip : (x2 + 1) * strip, :] = turned[first : first + strip]
     abuf[z, x, mine] = act_t[z]
-    pl.semaphore_wait(barrier, len(partners))
-
-    sends = []
-
-    def launch(copy):
-        copy.start()
-        sends.append(copy)
-
-    def c1(d):
-        j = lax.rem(x + d, nx)
-        return remote(
-            cot.at[:, pl.ds(pl.multiple_of(j * block, block), block)],
-            cbuf.at[z, x], c1_s.at[d - 1], c1_r.at[d - 1], x=j,
-        )
-
-    def a1(d):
-        z2 = lax.rem(z + d, nz)
-        return remote(act_t.at[z2], abuf.at[z, x, mine], a1_s.at[d - 1], a1_r.at[d - 1], z=z2)
-
-    def ring(way, hop, k):
-        x2 = lax.rem(x - k + nx, nx)
-        step = 1 if way == 0 else nz - 1
-        origin = lax.rem(z - hop + nz, nz) if way == 0 else lax.rem(z + hop, nz)
-        part = cbuf.at[origin, x2]
-        return remote(
-            part, part, zr_s.at[way, hop, k], zr_r.at[way, hop, k], z=lax.rem(z + step, nz)
-        )
-
-    def a2(d):
-        part = abuf.at[:, x, mine]
-        return remote(part, part, a2_s.at[d - 1], a2_r.at[d - 1], x=lax.rem(x + d, nx))
-
-    def over_y(k, d):
-        part = abuf.at[:, lax.rem(x - k + nx, nx), mine]
-        return remote(
-            part, part, y_s.at[k, d - 1], y_r.at[k, d - 1], y=lax.rem(y + d, ny)
-        )
-
-    def sibling(k, d):
-        part = abuf.at[:, lax.rem(x - k + nx, nx), 2 * lax.rem(y - d + ny, ny) + c]
-        return remote(part, part, sib_s.at[k, d], sib_r.at[k, d], c=1 - c)
-
-    near = [1, nx - 1]
-    for d in near:
-        c1(d).start()
-    own_c.wait()
-    for way in range(2):
-        launch(ring(way, 0, 0))
     for d in range(1, nz):
         launch(a1(d))
     for d in near:
@@ -160,6 +161,7 @@
     for d in range(1, ny):
         launch(over_y(0, d))
     launch(sibling(0, 0))
+    own_c.wait()
     for load in loads:
         load.wait()
 
@@ -624,32 +626,24 @@
 
 def settle_kernel(
     left, right, variance, direction, left_out, right_out, variance_out, direction_out,
-    held, taken, spread, turned, in_sem, out_sem, way_sem,
+    held, held_rows, taken, spread, turned, in_sem, out_sem, way_sem,
 ):
-    block = variance.shape[1]
-    count, strip = direction.shape[:2]
+    count, strip, block = direction.shape
     lane = spread.shape[2]
-    per, part = held.shape[0] // 5, held.shape[1]
-    pairs = []
-    for step in range(per):
-        rows = pl.ds(step * part, part)
-        for src, dst in ((left, left_out), (right, right_out)):
-            pairs += [(src.at[s, rows, :], dst.at[s, rows, :]) for s in range(2)]
-        pairs += [(variance.at[rows, :], variance_out.at[rows, :])]
+    pairs = [(left.at[k], held.at[k], left_out.at[k]) for k in range(2)]
+    pairs += [(right.at[k], held.at[2 + k], right_out.at[k]) for k in range(2)]
+    pairs += [(variance, held_rows, variance_out)]
     first = pltpu.make_async_copy(direction, taken, way_sem.at[0])
     last = pltpu.make_async_copy(turned, direction_out, way_sem.at[1])
     reads = [
-        pltpu.make_async_copy(src, held.at[k], in_sem.at[k]) for k, (src, _) in enumerate(pairs)
+        pltpu.make_async_copy(src, mid, in_sem.at[k]) for k, (src, mid, _) in enumerate(pairs)
     ]
     writes = [
-        pltpu.make_async_copy(held.at[k], dst, out_sem.at[k]) for k, (_, dst) in enumerate(pairs)
+        pltpu.make_async_copy(mid, dst, out_sem.at[k]) for k, (_, mid, dst) in enumerate(pairs)
     ]
     first.start()
     for copy in reads:
         copy.start()
-    for k in range(len(pairs) // 2):
-        reads[k].wait()
-        writes[k].start()
     first.wait()
     value = taken[...].reshape(count * strip, block).astype(jnp.float32)
     for k in range(block // lane):
@@ -659,9 +653,9 @@
             [spread[k, pl.ds(r, count, stride=strip), :] for k in range(block // lane)], axis=1
         ).astype(turned.dtype)
     last.start()
-    for k in range(len(pairs) // 2, len(pairs)):
-        reads[k].wait()
-        writes[k].start()
+    for read, write in zip(reads, writes):
+        read.wait()
+        write.start()
     for copy in writes:
         copy.wait()
     last.wait()
@@ -669,8 +663,7 @@
 
 def settle(left, right, variance, direction):
     count, strip, block = direction.shape
-    lane, part = min(block, 128), block // 4
-    pieces = 5 * (block // part)
+    lane = min(block, 128)
     anywhere = pl.BlockSpec(memory_space=pl.ANY)
     vmem, sem = pltpu.VMEM, pltpu.SemaphoreType.DMA
     return pl.pallas_call(
@@ -680,11 +673,12 @@
         in_specs=[anywhere] * 4,
         out_specs=(anywhere,) * 4,
         scratch_shapes=[
-            vmem((pieces, part, block), variance.dtype),
+            vmem((4, block, block), left.dtype),
+            vmem(variance.shape, variance.dtype),
             vmem(direction.shape, direction.dtype),
             vmem((block // lane, count * strip, lane), jnp.float32),
             vmem((strip, count, block), direction.dtype),
-            sem((pieces,)), sem((pieces,)), sem((2,)),
+            sem((5,)), sem((5,)), sem((2,)),
         ],
         compiler_params=pltpu.CompilerParams(vmem_limit_bytes=60 * 1024 * 1024),
     )(left, right, variance, direction)

time: 123 us -> 122 us (level)
  no operation moved by 1% of the time
where the time goes in v6:
time: 122 us
  Pallas kernels  121 us (99%)
    pallas_call x1, Pallas kernels, shampoo(): pl.pallas_call(functools.partial(step_kernel, sizes), out_shape=(jax.Shap...  116 us
    pallas_call x1, Pallas kernels, settle(): pl.pallas_call(settle_kernel, out_shape=tuple((jax.ShapeDtypeStruct(a.sha...  5.31 us

profile of v6, /device:TPU:8, one launch (start us, length us, event | category | flops | bytes accessed | tf_op | source)
XLA Modules:
  0.0 122.0 jit_solution(3282388792100960734)
XLA Ops:
  0.6 116.0 %shard_map.93 = (bf16[32,16,512]{2,1,0:T(8,128)(2,1)}, f32[2,512,512]{2,1,0:T(8,128)}, f32[2,512,512]{2,1,0:T(8,128)}, f32[512,512]{1,0:T(8,128)}) custom-call(bf16[128,512]{1,0:T(8,128)(2,1)} %act.1, bf16[128,2048]{1,0:T(8,128)(2,1)} %cot.1, f32[2,512,512]{2,1,0:T(8,128)} %bitcast.8, f32[2,512,512]{2,1,0:T(8,128)} %bitcast.9, f32[512,512]{1,0:T(8,128)} %bitcast.10, ...), custom_call_target="tpu_custom_call" | custom-call | tf_op jit(solution)/shard_map/pallas_call | solution.py:565
  116.7 5.3 %shard_map.94 = (f32[2,512,512]{2,1,0:T(8,128)}, f32[2,512,512]{2,1,0:T(8,128)}, f32[512,512]{1,0:T(8,128)}, bf16[16,32,512]{2,1,0:T(8,128)(2,1)}) custom-call(f32[2,512,512]{2,1,0:T(8,128)} %get-tuple-element.12.left, f32[2,512,512]{2,1,0:T(8,128)} %get-tuple-element.13.right, f32[512,512]{1,0:T(8,128)} %get-tuple-element.14.variance, ...), custom_call_target="tpu_custom_call" | custom-call | tf_op jit(solution)/shard_map/pallas_call | solution.py:669

commit v7 on v6

--- a/solution.py
+++ b/solution.py
@@ -23,14 +23,19 @@
     return jnp.dot(left, right, preferred_element_type=jnp.float32)
 
 
+def half_product(step, left_high, left_low, right_high, right_low, order, finish):
+    tile = order // 2
+    rows = pl.ds(step * tile, tile)
+    if not isinstance(step, int):
+        rows = pl.ds(pl.multiple_of(step * tile, tile), tile)
+    high, low = left_high[rows, :], left_low[rows, :]
+    total = dot(high, right_low[...]) + dot(low, right_high[...])
+    finish(rows, dot(high, right_high[...]) + total)
+
+
 def tiled_product(left_high, left_low, right_high, right_low, order, finish):
-    tile = order // 2
-
     def one(step, carry):
-        rows = pl.ds(pl.multiple_of(step * tile, tile), tile)
-        high, low = left_high[rows, :], left_low[rows, :]
-        total = dot(high, right_low[...]) + dot(low, right_high[...])
-        finish(rows, dot(high, right_high[...]) + total)
+        half_product(step, left_high, left_low, right_high, right_low, order, finish)
         return carry
 
     lax.fori_loop(0, 2, one, 0)
@@ -40,14 +45,18 @@
     sizes, act, cot, stats_left, stats_right, variance, owners,
     direction, left_new, right_new, var_new,
     act_in, act_t, source, targets, used, cbuf, abuf, grad, sbuf, vbuf, vt, matrix, m2, m_h, m_l, m2_h, m2_l, w_h, w_l, root_h, root_l,
-    gsend, gsend_row, gq, gq_row, scale_rows, adam_rows, send_q, send_row, rq, rq_row,
+    gsend, gsend_row, gq_first, gq_second, gq_row, scale_rows, adam_rows, send_q, send_both, send_row, rq, rq_both,
+    rq_row,
     owned_h, owned_l, pre, finished, ret,
     own_sem, stat_sem, out_sem, var_sem, c1_s, c1_r, a1_s, a1_r, zr_s, zr_r, a2_s, a2_r,
-    y_s, y_r, sib_s, sib_r, ex_s, ex_r, exr_s, exr_r, go_s, go_r, gor_s, gor_r, back_s, back_r,
+    y_s, y_r, sib_s, sib_r, ex_s, ex_r, exr_s, exr_r, go_s, go_r, both_s, both_r,
+    gor_s, gor_r, back_s, back_r,
 ):
     nx, nz, ny, block, strip, tokens, rows_i = sizes
     count, devices, width = rows_i * nx, nx * nz, rows_i * strip
     lane = vbuf.shape[2]
+    wide = block // 2
+    gq = (gq_first, gq_second)
     half = nz // 2
     x, z = lax.axis_index("x"), lax.axis_index("z")
     y, c = lax.axis_index("y"), lax.axis_index("c")
@@ -73,9 +82,13 @@
         for side, ref in enumerate((stats_left, stats_right))
         for slot in range(2)
     ]
-    own_c = pltpu.make_async_copy(
-        cot.at[:, pl.ds(pl.multiple_of(x * block, block), block)], cbuf.at[z, x], own_sem.at[0]
-    )
+
+    def columns(j, p):
+        return cot.at[:, pl.ds(pl.multiple_of(j * block + p * wide, wide), wide)]
+
+    own_c = [
+        pltpu.make_async_copy(columns(x, p), cbuf.at[p, z, x], own_sem.at[2 * p]) for p in range(2)
+    ]
     act_load = pltpu.make_async_copy(act, act_in, own_sem.at[1])
     loads += [
         pltpu.make_async_copy(
@@ -84,7 +97,8 @@
         for k in range(block // lane)
     ]
     act_load.start()
-    own_c.start()
+    for copy in own_c:
+        copy.start()
     for load in loads:
         load.start()
 
@@ -96,26 +110,23 @@
         copy.start()
         sends.append(copy)
 
-    def c1(d):
+    def c1(d, p):
         j = lax.rem(x + d, nx)
         return remote(
-            cot.at[:, pl.ds(pl.multiple_of(j * block, block), block)],
-            cbuf.at[z, x], c1_s.at[d - 1], c1_r.at[d - 1], x=j,
+            columns(j, p), cbuf.at[p, z, x], c1_s.at[p, d - 1], c1_r.at[p, d - 1], x=j
         )
 
     def a1(d):
         z2 = lax.rem(z + d, nz)
         return remote(act_t.at[z2], abuf.at[z, x, mine], a1_s.at[d - 1], a1_r.at[d - 1], z=z2)
 
-    own = cot.at[:, pl.ds(pl.multiple_of(x * block, block), block)]
-
-    def ring(way, hop, k, held=None):
+    def ring(way, hop, k, p, held=None):
         x2 = lax.rem(x - k + nx, nx)
         step = 1 if way == 0 else nz - 1
         origin = lax.rem(z - hop + nz, nz) if way == 0 else lax.rem(z + hop, nz)
-        part = cbuf.at[origin, x2]
+        part = cbuf.at[p, origin, x2]
         return remote(
-            part if held is None else held, part, zr_s.at[way, hop, k], zr_r.at[way, hop, k], z=lax.rem(z + step, nz)
+            part if held is None else held, part, zr_s.at[p, way, hop, k], zr_r.at[p, way, hop, k], z=lax.rem(z + step, nz)
         )
 
     def a2(d):
@@ -132,11 +143,11 @@
         part = abuf.at[:, lax.rem(x - k + nx, nx), 2 * lax.rem(y - d + ny, ny) + c]
         return remote(part, part, sib_s.at[k, d], sib_r.at[k, d], c=1 - c)
 
-    near = [1, nx - 1]
+    near, far_x = [1, nx - 1], list(range(2, nx - 1))
     for d in near:
-        c1(d).start()
+        c1(d, 0).start()
     for way in range(2):
-        launch(ring(way, 0, 0, own))
+        launch(ring(way, 0, 0, 0, columns(x, 0)))
     act_load.wait()
     turned = act_in[...].T
     for x2 in range(nx):
@@ -146,14 +157,19 @@
     abuf[z, x, mine] = act_t[z]
     for d in range(1, nz):
         launch(a1(d))
+    for way in range(2):
+        launch(ring(way, 0, 0, 1, columns(x, 1)))
     for d in near:
-        c1(d).wait_send()
-    for d in range(2, nx - 1):
-        launch(c1(d))
-    for k in near + list(range(2, nx - 1)):
-        c1(k).wait_recv()
-        for way in range(2):
-            launch(ring(way, 0, k))
+        c1(d, 0).wait_send()
+    for d in far_x:
+        launch(c1(d, 0))
+    for d in near + far_x:
+        launch(c1(d, 1))
+    for p in range(2):
+        for k in near + far_x:
+            c1(k, p).wait_recv()
+            for way in range(2):
+                launch(ring(way, 0, k, p))
     for d in range(1, nz):
         a1(d).wait_recv()
     for d in range(1, nx):
@@ -161,7 +177,8 @@
     for d in range(1, ny):
         launch(over_y(0, d))
     launch(sibling(0, 0))
-    own_c.wait()
+    for copy in own_c:
+        copy.wait()
     for load in loads:
         load.wait()
 
@@ -190,99 +207,8 @@
         used[slot] = jnp.where(held > slot, 1.0, 0.0)
 
     items = nx * (ny - 1)
-    per_step = -(-items // 6)
-
-    def one_matrix(q, carry):
-        for t in range(3):
-            n = 3 * q + t
-            hop, place = n // nx + 1, lax.rem(n, nx)
-            k = jnp.where(place == 2, nx - 1, jnp.where(place == 3, 2, place))
-            ring(0, hop - 1, k).wait_recv()
-            ring(1, hop - 1, k).wait_recv()
-            inner = hop < half - 1
-
-            @pl.when(jnp.logical_or(inner, place < nx // 2))
-            def _():
-                ring(0, hop, k).start()
-
-            @pl.when(jnp.logical_or(inner, place >= nx // 2))
-            def _():
-                ring(1, hop, k).start()
-
-            if t + 1 < nx:
-
-                @pl.when(q == 0)
-                def _():
-                    a2(t + 1).wait_recv()
-                    for d in range(1, ny):
-                        over_y(t + 1, d).start()
-                    sibling(t + 1, 0).start()
-
-            for extra in range(per_step):
-                item = (n - 3) * per_step + extra
-
-                @pl.when(jnp.logical_and(n >= 3, item < items))
-                def _():
-                    k2, d2 = item // (ny - 1), lax.rem(item, ny - 1) + 1
-                    over_y(k2, d2).wait_recv()
-                    sibling(k2, d2).start()
-
-            each = -(-devices // 12)
-            lax.fori_loop(n * each, jnp.minimum(n * each + each, devices), find_blocks, 0)
-            each = -(-count // 12)
-            lax.fori_loop(n * each, jnp.minimum(n * each + each, count), find_target, 0)
-
-            if t == 0:
-                stat = sbuf[q]
-                bound = jnp.max(jnp.sum(jnp.abs(stat), axis=1, keepdims=True), axis=0, keepdims=True)
-                value = stat * (1.0 / bound)
-                matrix[...] = value
-                m_h[...], m_l[...] = halves(value)
-
-                def finish(rows, value):
-                    m2[rows, :] = value
-                    m2_h[rows, :], m2_l[rows, :] = halves(value)
-                    w_h[rows, :], w_l[rows, :] = halves(
-                        COEFFICIENTS[5] * matrix[rows, :] + COEFFICIENTS[6] * value
-                    )
-
-                tiled_product(m_h, m_l, m_h, m_l, block, finish)
-            elif t == 1:
-
-                def finish(rows, value):
-                    value += COEFFICIENTS[3] * matrix[rows, :] + COEFFICIENTS[4] * m2[rows, :]
-                    m_h[rows, :], m_l[rows, :] = halves(value)
-
-                tiled_product(m2_h, m2_l, w_h, w_l, block, finish)
-            else:
-
-                def finish(rows, value):
-                    value += COEFFICIENTS[1] * matrix[rows, :] + COEFFICIENTS[2] * m2[rows, :]
-                    ids = lax.broadcasted_iota(jnp.int32, value.shape, 0) + rows.start
-                    columns = lax.broadcasted_iota(jnp.int32, value.shape, 1)
-                    value += jnp.where(ids == columns, COEFFICIENTS[0], 0.0)
-                    root_h[q, rows, :], root_l[q, rows, :] = halves(value)
-
-                tiled_product(m2_h, m2_l, m_h, m_l, block, finish)
-
-            each = -(-count // 12)
-            for extra in range(each):
-                b = n * each + extra
-
-                @pl.when(b < count)
-                def _():
-                    rows = pl.ds(pl.multiple_of(b * strip, strip), strip)
-                    for k in range(block // lane):
-                        vt[k, rows, :] = vbuf[k, pl.ds(b, strip, stride=count), :]
-        return carry
-
-    lax.fori_loop(0, 4, one_matrix, 0)
-
-    for k in range(nx):
-        for d in range(ny):
-            sibling(k, d).wait_recv()
-
-    def shard(origin, rows=None):
+
+    def shard(origin, p, rows=None):
         parts = []
         for x2 in range(nx):
             if rows is None:
@@ -291,72 +217,177 @@
                 piece = abuf[origin, x2, :, rows, :]
             parts.append(piece.reshape(-1, tokens))
         left = jnp.concatenate(parts, axis=1)
-        return dot(left, cbuf[origin].reshape(nx * tokens, block))
-
-    grad[...] = shard(z).reshape(grad.shape)
-
-    def add(d, carry):
-        grad[...] += shard(lax.rem(z + d + (d >= half).astype(jnp.int32), nz)).reshape(grad.shape)
-        return carry
-
-    lax.fori_loop(1, nz - 1, add, 0)
-
-    for k in range(nx):
-        ring(0 if k < nx // 2 else 1, half - 1, k).wait_recv()
-    far = lax.rem(z + half, nz)
-
-    def exchange(d):
-        j = lax.rem(x + d, nx)
-        return (
-            remote(gsend.at[j], gq.at[x], ex_s.at[d - 1], ex_r.at[d - 1], x=j),
-            remote(gsend_row.at[j], gq_row.at[x], exr_s.at[d - 1], exr_r.at[d - 1], x=j),
-        )
+        return dot(left, cbuf[p, origin].reshape(nx * tokens, wide))
 
     diagonal = lax.broadcasted_iota(jnp.int32, (width, width), 0) == lax.broadcasted_iota(
         jnp.int32, (width, width), 1
     )
-    for d in [2, 1, nx - 1, 0]:
+
+    def exchange(d, p):
         j = lax.rem(x + d, nx)
-        rows = pl.ds(pl.multiple_of(j * strip, strip), strip)
-        value = grad[:, rows, :].reshape(width, block) + shard(far, rows)
-        top = jnp.maximum(jnp.max(jnp.abs(value), axis=1, keepdims=True), 1e-30)
-        coded = jnp.round(value * (32767.0 / top)).astype(jnp.int32).astype(jnp.int16)
-        row = jnp.sum(jnp.where(diagonal, top * (1.0 / 32767.0), 0.0), axis=0, keepdims=True)
-        if d:
-            gsend[j] = coded.reshape(rows_i, strip, block)
-            gsend_row[j] = row
-            for copy in exchange(d):
-                launch(copy)
-        else:
-            gq[x] = coded.reshape(rows_i, strip, block)
-            gq_row[x] = row
+        return (
+            remote(gsend.at[p, j], gq[p].at[x], ex_s.at[p, d - 1], ex_r.at[p, d - 1], x=j),
+            remote(
+                gsend_row.at[p, j], gq_row.at[p, x], exr_s.at[p, d - 1], exr_r.at[p, d - 1], x=j
+            ),
+        )
+
+    def finish_columns(p):
+        grad[...] = shard(z, p).reshape(grad.shape)
+
+        def add(d, carry):
+            origin = lax.rem(z + d + (d >= half).astype(jnp.int32), nz)
+            grad[...] += shard(origin, p).reshape(grad.shape)
+            return carry
+
+        lax.fori_loop(1, nz - 1, add, 0)
+        for k in range(nx):
+            ring(0 if k < nx // 2 else 1, half - 1, k, p).wait_recv()
+        far = lax.rem(z + half, nz)
+        for d in [2, 1, nx - 1, 0]:
+            j = lax.rem(x + d, nx)
+            rows = pl.ds(pl.multiple_of(j * strip, strip), strip)
+            value = grad[:, rows, :].reshape(width, wide) + shard(far, p, rows)
+            top = jnp.maximum(jnp.max(jnp.abs(value), axis=1, keepdims=True), 1e-30)
+            coded = jnp.round(value * (32767.0 / top)).astype(jnp.int32).astype(jnp.int16)
+            row = jnp.sum(jnp.where(diagonal, top * (1.0 / 32767.0), 0.0), axis=0, keepdims=True)
+            if d:
+                gsend[p, j] = coded.reshape(rows_i, strip, wide)
+                gsend_row[p, j] = row
+                for copy in exchange(d, p):
+                    copy.start()
+            else:
+                gq[p][x] = coded.reshape(rows_i, strip, wide)
+                gq_row[p, x] = row
+
+    def one_matrix(q, carry):
+        p = (q >= 2).astype(jnp.int32)
+        for u in range(6):
+            t, tile = u // 2, u % 2
+            n = 6 * q + u
+            inner_n = n - 12 * p
+            hop, place = inner_n // nx + 1, lax.rem(inner_n, nx)
+            k = jnp.where(place == 2, nx - 1, jnp.where(place == 3, 2, place))
+            ring(0, hop - 1, k, p).wait_recv()
+            ring(1, hop - 1, k, p).wait_recv()
+            inner = hop < half - 1
+
+            @pl.when(jnp.logical_or(inner, place < nx // 2))
+            def _():
+                ring(0, hop, k, p).start()
+
+            @pl.when(jnp.logical_or(inner, place >= nx // 2))
+            def _():
+                ring(1, hop, k, p).start()
+
+            if u + 1 < nx:
+
+                @pl.when(q == 0)
+                def _():
+                    a2(u + 1).wait_recv()
+                    for d in range(1, ny):
+                        over_y(u + 1, d).start()
+                    sibling(u + 1, 0).start()
+
+            item = n - 5
+            if ny > 1:
+
+                @pl.when(jnp.logical_and(item >= 0, item < items))
+                def _():
+                    k2, d2 = item // (ny - 1), lax.rem(item, ny - 1) + 1
+                    over_y(k2, d2).wait_recv()
+                    sibling(k2, d2).start()
+
+            if u == 2:
+
+                @pl.when(q == 3)
+                def _():
+                    for k3 in range(nx):
+                        for d in range(ny):
+                            sibling(k3, d).wait_recv()
+                    finish_columns(0)
+
+            each = -(-devices // 24)
+            lax.fori_loop(n * each, jnp.minimum(n * each + each, devices), find_blocks, 0)
+            each = -(-count // 24)
+            lax.fori_loop(n * each, jnp.minimum(n * each + each, count), find_target, 0)
+
+            if t == 0:
+                if tile == 0:
+                    stat = sbuf[q]
+                    bound = jnp.max(
+                        jnp.sum(jnp.abs(stat), axis=1, keepdims=True), axis=0, keepdims=True
+                    )
+                    value = stat * (1.0 / bound)
+                    matrix[...] = value
+                    m_h[...], m_l[...] = halves(value)
+
+                def finish(rows, value):
+                    m2[rows, :] = value
+                    m2_h[rows, :], m2_l[rows, :] = halves(value)
+                    w_h[rows, :], w_l[rows, :] = halves(
+                        COEFFICIENTS[5] * matrix[rows, :] + COEFFICIENTS[6] * value
+                    )
+
+                half_product(tile, m_h, m_l, m_h, m_l, block, finish)
+            elif t == 1:
+
+                def finish(rows, value):
+                    value += COEFFICIENTS[3] * matrix[rows, :] + COEFFICIENTS[4] * m2[rows, :]
+                    m_h[rows, :], m_l[rows, :] = halves(value)
+
+                half_product(tile, m2_h, m2_l, w_h, w_l, block, finish)
+            else:
+
+                def finish(rows, value):
+                    value += COEFFICIENTS[1] * matrix[rows, :] + COEFFICIENTS[2] * m2[rows, :]
+                    ids = lax.broadcasted_iota(jnp.int32, value.shape, 0) + rows.start
+                    columns = lax.broadcasted_iota(jnp.int32, value.shape, 1)
+                    value += jnp.where(ids == columns, COEFFICIENTS[0], 0.0)
+                    root_h[q, rows, :], root_l[q, rows, :] = halves(value)
+
+                half_product(tile, m2_h, m2_l, m_h, m_l, block, finish)
+
+            each = -(-count // 24)
+            for extra in range(each):
+                b = n * each + extra
+
+                @pl.when(b < count)
+                def _():
+                    rows = pl.ds(pl.multiple_of(b * strip, strip), strip)
+                    for k in range(block // lane):
+                        vt[k, rows, :] = vbuf[k, pl.ds(b, strip, stride=count), :]
+        return carry
+
+    lax.fori_loop(0, 4, one_matrix, 0)
 
     lanes = lax.broadcasted_iota(jnp.int32, (1, width), 1)
 
-    def strips_of(j):
-        row = gq_row[j]
+    def strips_of(j, p):
+        row = gq_row[p, j]
         column = jnp.sum(jnp.where(diagonal, row, 0.0), axis=1, keepdims=True)
+        chunks = range(p * wide // lane, (p + 1) * wide // lane)
         for i in range(rows_i):
             b = i * nx + j
-            value = gq[j, i].astype(jnp.float32) * column[i * strip : (i + 1) * strip]
+            value = gq[p][j, i].astype(jnp.float32) * column[i * strip : (i + 1) * strip]
             square = value * value
             rows = pl.ds(pl.multiple_of(b * strip, strip), strip)
-            old = jnp.concatenate([vt[k, rows, :] for k in range(block // lane)], axis=1)
+            old = jnp.concatenate([vt[k, rows, :] for k in chunks], axis=1)
             fresh = 0.9 * old + 0.1 * square
-            for k in range(block // lane):
-                vt[k, rows, :] = fresh[:, k * lane : (k + 1) * lane]
+            for at, k in enumerate(chunks):
+                vt[k, rows, :] = fresh[:, at * lane : (at + 1) * lane]
             total = jnp.sum(square / fresh, axis=0, keepdims=True)
-            adam_rows[pl.ds(b, 1), :] = sum(
-                total[:, k * width : (k + 1) * width] for k in range(block // width)
-            )
+            folded = sum(total[:, k * width : (k + 1) * width] for k in range(wide // width))
             inside = jnp.logical_and(lanes >= i * strip, lanes < (i + 1) * strip)
-            scale_rows[pl.ds(b, 1), :] = jnp.where(inside, row, 0.0)
-
-    strips_of(x)
-    for d in (1, nx - 1, 2):
-        for copy in exchange(d):
-            copy.wait_recv()
-        strips_of(lax.rem(x - d + nx, nx))
+            adam_rows[p, pl.ds(b, 1), :] = folded
+            scale_rows[p, pl.ds(b, 1), :] = jnp.where(inside, row, 0.0)
+
+    def strips_half(p):
+        strips_of(x, p)
+        for d in (1, nx - 1, 2):
+            for copy in exchange(d, p):
+                copy.wait_recv()
+            strips_of(lax.rem(x - d + nx, nx), p)
 
     def wrapped(value, size):
         return jnp.where(value >= size, value - size, value)
@@ -385,37 +416,57 @@
             go_s.at[slot, d - 1], go_r.at[slot, d - 1], x=x2, z=z2,
         )
 
+    def go_both(d, x2, z2):
+        return remote(
+            send_both.at[x2 * nz + z2], rq_both.at[me],
+            both_s.at[d - 1], both_r.at[d - 1], x=x2, z=z2,
+        )
+
     def go_row(d, x2, z2):
         return remote(
             send_row.at[x2 * nz + z2], rq_row.at[me], gor_s.at[d - 1], gor_r.at[d - 1], x=x2, z=z2
         )
 
-    def picked(slot, other):
+    def picked(slot, other, p):
         b = source[2 * other + slot]
-        return gq[lax.rem(b, nx), b // nx]
+        return gq[p][lax.rem(b, nx), b // nx]
 
     def picked_rows(other):
         return jnp.concatenate(
             [
-                rows[pl.ds(source[2 * other + slot], 1), :]
+                rows[p, pl.ds(source[2 * other + slot], 1), :]
                 for slot in range(2)
                 for rows in (scale_rows, adam_rows)
+                for p in range(2)
             ],
             axis=0,
         )
 
+    strips_half(0)
+
+    def send_first(d, x2, z2):
+        other = x2 * nz + z2
+        for slot in range(2):
+            send_both[other, slot] = picked(slot, other, 0)
+        go_both(d, x2, z2).start()
+
+    others(send_first, 1)
+    for slot in range(2):
+        rq_both[me, slot] = picked(slot, me, 0)
+    finish_columns(1)
+    strips_half(1)
     for slot in range(2):
 
         def send(d, x2, z2):
             other = x2 * nz + z2
-            send_q[slot, other] = picked(slot, other)
-            go(slot, d, x2, z2).start()
+            send_q[slot, other] = picked(slot, other, 1)
             if slot == 0:
                 send_row[other] = picked_rows(other)
                 go_row(d, x2, z2).start()
+            go(slot, d, x2, z2).start()
 
         others(send, 1)
-        rq[slot, me] = picked(slot, me)
+        rq[slot, me] = picked(slot, me, 1)
         if slot == 0:
             rq_row[me] = picked_rows(me)
 
@@ -448,22 +499,29 @@
     for slot in range(2):
         keep = used[slot]
 
-        def decode(p):
-            row = rq_row[p, 2 * slot : 2 * slot + 1]
-            column = jnp.sum(jnp.where(fits, row, 0.0), axis=1, keepdims=True) * keep
-            value = rq[slot, p].astype(jnp.float32) * column
-            rows = pl.ds(pl.multiple_of(p * strip, strip), strip)
+        def decode(other):
+            values = []
+            for p, data in enumerate((rq_both[other, slot], rq[slot, other])):
+                row = rq_row[other, 4 * slot + p : 4 * slot + p + 1]
+                column = jnp.sum(jnp.where(fits, row, 0.0), axis=1, keepdims=True) * keep
+                values.append(data.astype(jnp.float32) * column)
+            rows = pl.ds(pl.multiple_of(other * strip, strip), strip)
+            value = jnp.concatenate(values, axis=1)
             owned_h[slot, rows, :], owned_l[slot, rows, :] = halves(value)
 
         def receive(d, x2, z2):
             if slot == 0:
+                go_both(d, x2, z2).wait_recv()
                 go_row(d, x2, z2).wait_recv()
             go(slot, d, x2, z2).wait_recv()
             decode(x2 * nz + z2)
 
         decode(me)
         others(receive, -1)
-        total = jnp.sum(rq_row[:, 2 * slot + 1 : 2 * slot + 2, :], axis=0)
+        total = jnp.sum(
+            rq_row[:, 4 * slot + 2 : 4 * slot + 3, :] + rq_row[:, 4 * slot + 3 : 4 * slot + 4, :],
+            axis=0,
+        )
 
         def finish(rows, value):
             m_h[rows, :], m_l[rows, :] = halves(value)
@@ -530,13 +588,19 @@
         others(lambda d, x2, z2: go(slot, d, x2, z2).wait_send(), 1)
         others(lambda d, x2, z2: back(slot, d, x2, z2).wait_send(), 1)
     others(lambda d, x2, z2: go_row(d, x2, z2).wait_send(), 1)
+    others(lambda d, x2, z2: go_both(d, x2, z2).wait_send(), 1)
+    for p in range(2):
+        for d in range(1, nx):
+            for copy in exchange(d, p):
+                copy.wait_send()
     for copy in sends:
         copy.wait_send()
-    for hop in range(1, half):
-        for k in range(nx):
-            for way in range(2):
-                if hop < half - 1 or (k < nx // 2) == (way == 0):
-                    ring(way, hop, k).wait_send()
+    for p in range(2):
+        for hop in range(1, half):
+            for k in range(nx):
+                for way in range(2):
+                    if hop < half - 1 or (k < nx // 2) == (way == 0):
+                        ring(way, hop, k, p).wait_send()
     for k in range(1, nx):
         for d in range(1, ny):
             over_y(k, d).wait_send()
@@ -556,7 +620,8 @@
     sizes = (nx, nz, ny, block, strip, tokens, rows_i)
     half = nz // 2
     count, devices, width = rows_i * nx, nx * nz, rows_i * strip
-    lane = min(block, 128)
+    lane = min(block // 2, 128)
+    wide = block // 2
     bf16, f32, i16 = jnp.bfloat16, jnp.float32, jnp.int16
     sem, vmem = pltpu.SemaphoreType.DMA, pltpu.VMEM
     square = (block, block)
@@ -578,9 +643,9 @@
             pltpu.SMEM((2 * devices,), jnp.int32),
             pltpu.SMEM((count,), jnp.int32),
             pltpu.SMEM((2,), f32),
-            vmem((nz, nx, tokens, block), bf16),
+            vmem((2, nz, nx, tokens, wide), bf16),
             vmem((nz, nx, rows_i, rows_z, tokens), bf16),
-            vmem((rows_i, rows_z, block), f32),
+            vmem((rows_i, rows_z, wide), f32),
             vmem((4, block, block), f32),
             vmem((block // lane, strip * count, lane), f32),
             vmem((block // lane, strip * count, lane), f32),
@@ -591,32 +656,35 @@
         + [
             vmem((4, block, block), bf16),
             vmem((4, block, block), bf16),
-            vmem((nx, rows_i, strip, block), i16),
-            vmem((nx, 1, width), f32),
-            vmem((nx, rows_i, strip, block), i16),
-            vmem((nx, 1, width), f32),
-            vmem((count, width), f32),
-            vmem((count, width), f32),
-            vmem((2, devices, strip, block), i16),
-            vmem((devices, 4, width), f32),
-            vmem((2, devices, strip, block), i16),
-            vmem((devices, 4, width), f32),
+            vmem((2, nx, rows_i, strip, wide), i16),
+            vmem((2, nx, 1, width), f32),
+            vmem((nx, rows_i, strip, wide), i16),
+            vmem((nx, rows_i, strip, wide), i16),
+            vmem((2, nx, 1, width), f32),
+            vmem((2, count, width), f32),
+            vmem((2, count, width), f32),
+            vmem((2, devices, strip, wide), i16),
+            vmem((devices, 2, strip, wide), i16),
+            vmem((devices, 8, width), f32),
+            vmem((2, devices, strip, wide), i16),
+            vmem((devices, 2, strip, wide), i16),
+            vmem((devices, 8, width), f32),
             vmem((2, block, block), bf16),
             vmem((2, block, block), bf16),
             vmem(square, f32),
             vmem((2, block, block), bf16),
             vmem((2 * devices, strip, block), bf16),
-            sem((2,)), sem((4,)), sem((4,)), sem((2, block // lane)),
-            sem((nx - 1,)), sem((nx - 1,)),
+            sem((3,)), sem((4,)), sem((4,)), sem((2, block // lane)),
+            sem((2, nx - 1)), sem((2, nx - 1)),
             sem((nz - 1,)), sem((nz - 1,)),
-            sem((2, half, nx)), sem((2, half, nx)),
+            sem((2, 2, half, nx)), sem((2, 2, half, nx)),
             sem((nx - 1,)), sem((nx - 1,)),
             sem((nx, max(1, ny - 1))), sem((nx, max(1, ny - 1))),
             sem((nx, ny)), sem((nx, ny)),
         ]
-        + [sem((nx - 1,))] * 4
+        + [sem((2, nx - 1))] * 4
         + [sem((2, devices - 1))] * 2
-        + [sem((devices - 1,))] * 2
+        + [sem((devices - 1,))] * 4
         + [sem((2, devices - 1))] * 2,
         compiler_params=pltpu.CompilerParams(
             collective_id=0, has_side_effects=True, vmem_limit_bytes=60 * 1024 * 1024

time: 122 us -> 118 us (0.967)
  Pallas kernels: 121 us -> 117 us
    pallas_call x1, Pallas kernels: 116 us -> 112 us  [shampoo(): pl.pallas_call(functools.partial(step_kernel, sizes), out_shape=(jax.Shap...]
where the time goes in v7:
time: 118 us
  Pallas kernels  117 us (99%)
    pallas_call x1, Pallas kernels, shampoo(): pl.pallas_call(functools.partial(step_kernel, sizes), out_shape=(jax.Shap...  112 us
    pallas_call x1, Pallas kernels, settle(): pl.pallas_call(settle_kernel, out_shape=tuple((jax.ShapeDtypeStruct(a.sha...  5.31 us

profile of v7, /device:TPU:8, one launch (start us, length us, event | category | flops | bytes accessed | tf_op | source)
XLA Modules:
  0.0 117.7 jit_solution(1905668015807769259)
XLA Ops:
  0.6 111.7 %shard_map.93 = (bf16[32,16,512]{2,1,0:T(8,128)(2,1)}, f32[2,512,512]{2,1,0:T(8,128)}, f32[2,512,512]{2,1,0:T(8,128)}, f32[512,512]{1,0:T(8,128)}) custom-call(bf16[128,512]{1,0:T(8,128)(2,1)} %act.1, bf16[128,2048]{1,0:T(8,128)(2,1)} %cot.1, f32[2,512,512]{2,1,0:T(8,128)} %bitcast.8, f32[2,512,512]{2,1,0:T(8,128)} %bitcast.9, f32[512,512]{1,0:T(8,128)} %bitcast.10, ...), custom_call_target="tpu_custom_call" | custom-call | tf_op jit(solution)/shard_map/pallas_call | solution.py:630
  112.4 5.3 %shard_map.94 = (f32[2,512,512]{2,1,0:T(8,128)}, f32[2,512,512]{2,1,0:T(8,128)}, f32[512,512]{1,0:T(8,128)}, bf16[16,32,512]{2,1,0:T(8,128)(2,1)}) custom-call(f32[2,512,512]{2,1,0:T(8,128)} %get-tuple-element.12.left, f32[2,512,512]{2,1,0:T(8,128)} %get-tuple-element.13.right, f32[512,512]{1,0:T(8,128)} %get-tuple-element.14.variance, ...), custom_call_target="tpu_custom_call" | custom-call | tf_op jit(solution)/shard_map/pallas_call | solution.py:737

commit v8 on v7

--- a/solution.py
+++ b/solution.py
@@ -45,7 +45,7 @@
     sizes, act, cot, stats_left, stats_right, variance, owners,
     direction, left_new, right_new, var_new,
     act_in, act_t, source, targets, used, cbuf, abuf, grad, sbuf, vbuf, vt, matrix, m2, m_h, m_l, m2_h, m2_l, w_h, w_l, root_h, root_l,
-    gsend, gsend_row, gq_first, gq_second, gq_row, scale_rows, adam_rows, send_q, send_both, send_row, rq, rq_both,
+    gsend, gsend_row, gq_first, gq_second, gq_row, scale_rows, send_q, send_both, send_row, rq, rq_both,
     rq_row,
     owned_h, owned_l, pre, finished, ret,
     own_sem, stat_sem, out_sem, var_sem, c1_s, c1_r, a1_s, a1_r, zr_s, zr_r, a2_s, a2_r,
@@ -377,10 +377,13 @@
             for at, k in enumerate(chunks):
                 vt[k, rows, :] = fresh[:, at * lane : (at + 1) * lane]
             total = jnp.sum(square / fresh, axis=0, keepdims=True)
-            folded = sum(total[:, k * width : (k + 1) * width] for k in range(wide // width))
-            inside = jnp.logical_and(lanes >= i * strip, lanes < (i + 1) * strip)
-            adam_rows[p, pl.ds(b, 1), :] = folded
-            scale_rows[p, pl.ds(b, 1), :] = jnp.where(inside, row, 0.0)
+            total = jnp.sum(total, axis=1, keepdims=True)
+            inside = jnp.logical_and(lanes >= p * strip, lanes < (p + 1) * strip)
+            moved = pltpu.roll(row, (p - i) * strip % width, 1)
+            packed = jnp.where(inside, moved, 0.0) + jnp.where(lanes == width - 1, total, 0.0)
+            if p:
+                packed += scale_rows[pl.ds(b, 1), :]
+            scale_rows[pl.ds(b, 1), :] = packed
 
     def strips_half(p):
         strips_of(x, p)
@@ -433,13 +436,7 @@
 
     def picked_rows(other):
         return jnp.concatenate(
-            [
-                rows[p, pl.ds(source[2 * other + slot], 1), :]
-                for slot in range(2)
-                for rows in (scale_rows, adam_rows)
-                for p in range(2)
-            ],
-            axis=0,
+            [scale_rows[pl.ds(source[2 * other + slot], 1), :] for slot in range(2)], axis=0
         )
 
     strips_half(0)
@@ -493,17 +490,19 @@
             back_s.at[slot, d - 1], back_r.at[slot, d - 1], x=x2, z=z2,
         )
 
-    fits = lax.rem(lax.broadcasted_iota(jnp.int32, (strip, width), 1), strip) == (
-        lax.broadcasted_iota(jnp.int32, (strip, width), 0)
-    )
+    fits = [
+        lax.broadcasted_iota(jnp.int32, (strip, width), 1)
+        == lax.broadcasted_iota(jnp.int32, (strip, width), 0) + p * strip
+        for p in range(2)
+    ]
     for slot in range(2):
         keep = used[slot]
 
         def decode(other):
             values = []
             for p, data in enumerate((rq_both[other, slot], rq[slot, other])):
-                row = rq_row[other, 4 * slot + p : 4 * slot + p + 1]
-                column = jnp.sum(jnp.where(fits, row, 0.0), axis=1, keepdims=True) * keep
+                row = rq_row[other, slot : slot + 1]
+                column = jnp.sum(jnp.where(fits[p], row, 0.0), axis=1, keepdims=True) * keep
                 values.append(data.astype(jnp.float32) * column)
             rows = pl.ds(pl.multiple_of(other * strip, strip), strip)
             value = jnp.concatenate(values, axis=1)
@@ -518,10 +517,8 @@
 
         decode(me)
         others(receive, -1)
-        total = jnp.sum(
-            rq_row[:, 4 * slot + 2 : 4 * slot + 3, :] + rq_row[:, 4 * slot + 3 : 4 * slot + 4, :],
-            axis=0,
-        )
+        total = jnp.sum(rq_row[:, slot : slot + 1, :], axis=0)
+        total = jnp.where(lanes == width - 1, total, 0.0)
 
         def finish(rows, value):
             m_h[rows, :], m_l[rows, :] = halves(value)
@@ -574,19 +571,7 @@
             copy.start()
 
     for slot in range(2):
-        others(lambda d, x2, z2: back(slot, d, x2, z2).wait_recv(), -1)
-
-    def choose(b, carry):
-        direction[b] = ret[targets[b]]
-        return carry
-
-    lax.fori_loop(0, count, choose, 0)
-
-    for copy in outs:
-        copy.wait()
-    for slot in range(2):
         others(lambda d, x2, z2: go(slot, d, x2, z2).wait_send(), 1)
-        others(lambda d, x2, z2: back(slot, d, x2, z2).wait_send(), 1)
     others(lambda d, x2, z2: go_row(d, x2, z2).wait_send(), 1)
     others(lambda d, x2, z2: go_both(d, x2, z2).wait_send(), 1)
     for p in range(2):
@@ -608,6 +593,19 @@
         for d in range(ny):
             if (k, d) != (0, 0):
                 sibling(k, d).wait_send()
+
+    for slot in range(2):
+        others(lambda d, x2, z2: back(slot, d, x2, z2).wait_recv(), -1)
+        others(lambda d, x2, z2: back(slot, d, x2, z2).wait_send(), 1)
+
+    def choose(b, carry):
+        direction[b] = ret[targets[b]]
+        return carry
+
+    lax.fori_loop(0, count, choose, 0)
+
+    for copy in outs:
+        copy.wait()
 
 
 def shampoo(act, cot, stats_left, stats_right, variance, owners):
@@ -661,14 +659,13 @@
             vmem((nx, rows_i, strip, wide), i16),
             vmem((nx, rows_i, strip, wide), i16),
             vmem((2, nx, 1, width), f32),
-            vmem((2, count, width), f32),
-            vmem((2, count, width), f32),
+            vmem((count, width), f32),
             vmem((2, devices, strip, wide), i16),
             vmem((devices, 2, strip, wide), i16),
-            vmem((devices, 8, width), f32),
+            vmem((devices, 2, width), f32),
             vmem((2, devices, strip, wide), i16),
             vmem((devices, 2, strip, wide), i16),
-            vmem((devices, 8, width), f32),
+            vmem((devices, 2, width), f32),
             vmem((2, block, block), bf16),
             vmem((2, block, block), bf16),
             vmem(square, f32),

time: 118 us -> 116 us (0.983)
  Pallas kernels: 117 us -> 115 us
    pallas_call x1, Pallas kernels: 112 us -> 109 us  [shampoo(): pl.pallas_call(functools.partial(step_kernel, sizes), out_shape=(jax.Shap...]
where the time goes in v8:
time: 116 us; the launch traced here: 115 us
  Pallas kernels  115 us (99%)
    pallas_call x1, Pallas kernels, shampoo(): pl.pallas_call(functools.partial(step_kernel, sizes), out_shape=(jax.Shap...  109 us
    pallas_call x1, Pallas kernels, settle(): pl.pallas_call(settle_kernel, out_shape=tuple((jax.ShapeDtypeStruct(a.sha...  5.31 us

profile of v8, /device:TPU:8, one launch (start us, length us, event | category | flops | bytes accessed | tf_op | source)
XLA Modules:
  0.0 115.4 jit_solution(13644341150313419637)
XLA Ops:
  0.6 109.5 %shard_map.93 = (bf16[32,16,512]{2,1,0:T(8,128)(2,1)}, f32[2,512,512]{2,1,0:T(8,128)}, f32[2,512,512]{2,1,0:T(8,128)}, f32[512,512]{1,0:T(8,128)}) custom-call(bf16[128,512]{1,0:T(8,128)(2,1)} %act.1, bf16[128,2048]{1,0:T(8,128)(2,1)} %cot.1, f32[2,512,512]{2,1,0:T(8,128)} %bitcast.8, f32[2,512,512]{2,1,0:T(8,128)} %bitcast.9, f32[512,512]{1,0:T(8,128)} %bitcast.10, ...), custom_call_target="tpu_custom_call" | custom-call | tf_op jit(solution)/shard_map/pallas_call | solution.py:628
  110.1 5.3 %shard_map.94 = (f32[2,512,512]{2,1,0:T(8,128)}, f32[2,512,512]{2,1,0:T(8,128)}, f32[512,512]{1,0:T(8,128)}, bf16[16,32,512]{2,1,0:T(8,128)(2,1)}) custom-call(f32[2,512,512]{2,1,0:T(8,128)} %get-tuple-element.12.left, f32[2,512,512]{2,1,0:T(8,128)} %get-tuple-element.13.right, f32[512,512]{1,0:T(8,128)} %get-tuple-element.14.variance, ...), custom_call_target="tpu_custom_call" | custom-call | tf_op jit(solution)/shard_map/pallas_call | solution.py:734

commit v9 on v8

--- a/solution.py
+++ b/solution.py
@@ -709,6 +709,9 @@
     first.start()
     for copy in reads:
         copy.start()
+    for read, write in zip(reads[:2], writes[:2]):
+        read.wait()
+        write.start()
     first.wait()
     value = taken[...].reshape(count * strip, block).astype(jnp.float32)
     for k in range(block // lane):
@@ -718,7 +721,7 @@
             [spread[k, pl.ds(r, count, stride=strip), :] for k in range(block // lane)], axis=1
         ).astype(turned.dtype)
     last.start()
-    for read, write in zip(reads, writes):
+    for read, write in zip(reads[2:], writes[2:]):
         read.wait()
         write.start()
     for copy in writes:

time: 116 us -> 115 us (level)
  no operation moved by 1% of the time
where the time goes in v9:
time: 115 us
  Pallas kernels  115 us (100%)
    pallas_call x1, Pallas kernels, shampoo(): pl.pallas_call(functools.partial(step_kernel, sizes), out_shape=(jax.Shap...  109 us
    pallas_call x1, Pallas kernels, settle(): pl.pallas_call(settle_kernel, out_shape=tuple((jax.ShapeDtypeStruct(a.sha...  5.07 us

profile of v9, /device:TPU:8, one launch (start us, length us, event | category | flops | bytes accessed | tf_op | source)
XLA Modules:
  0.0 115.2 jit_solution(5677569536896230988)
XLA Ops:
  0.6 109.5 %shard_map.93 = (bf16[32,16,512]{2,1,0:T(8,128)(2,1)}, f32[2,512,512]{2,1,0:T(8,128)}, f32[2,512,512]{2,1,0:T(8,128)}, f32[512,512]{1,0:T(8,128)}) custom-call(bf16[128,512]{1,0:T(8,128)(2,1)} %act.1, bf16[128,2048]{1,0:T(8,128)(2,1)} %cot.1, f32[2,512,512]{2,1,0:T(8,128)} %bitcast.8, f32[2,512,512]{2,1,0:T(8,128)} %bitcast.9, f32[512,512]{1,0:T(8,128)} %bitcast.10, ...), custom_call_target="tpu_custom_call" | custom-call | tf_op jit(solution)/shard_map/pallas_call | solution.py:628
  110.1 5.1 %shard_map.94 = (f32[2,512,512]{2,1,0:T(8,128)}, f32[2,512,512]{2,1,0:T(8,128)}, f32[512,512]{1,0:T(8,128)}, bf16[16,32,512]{2,1,0:T(8,128)(2,1)}) custom-call(f32[2,512,512]{2,1,0:T(8,128)} %get-tuple-element.12.left, f32[2,512,512]{2,1,0:T(8,128)} %get-tuple-element.13.right, f32[512,512]{1,0:T(8,128)} %get-tuple-element.14.variance, ...), custom_call_target="tpu_custom_call" | custom-call | tf_op jit(solution)/shard_map/pallas_call | solution.py:737
